TPU v7x, 256 devices: a whole 4x4x8 slice. The times are simulated.
256 devices in a mesh: tm: 8 (over z_lo, x), rows: 32 (over z_hi, y, core).
Axes of the slice: x: 4, y: 4, z: 8 (z_hi: 4, z_lo: 2; z = z_hi * 2 + z_lo), core: 2. Of those that a mesh axis runs over, the one named last changes fastest.
Arguments:
- noisy_frames: bfloat16 [3, 128, 256, 128], P(None, 'tm', 'rows'), may hold values from -6 to 6
- base_queue: bfloat16 [128, 3, 32, 16], P('tm', None, 'rows'), may hold values from -6 to 6
- frame_slot: int32 [128], replicated, may hold values from 0 to 127, each once
- blend_weight: int32 [128, 2], P('tm'), may hold values from 1 to 8
- weight_in: bfloat16 [3, 3, 6, 128], replicated, may hold values from -0.875 to 0.875
- bias_in: float32 [128], replicated, may hold values from -3 to 3
- gain_mid: float32 [128], replicated, may hold values from 0.1 to 1.9
- weight_mid: bfloat16 [3, 3, 128, 128], replicated, may hold values from -0.1875 to 0.1875
- time_mix: bfloat16 [128, 16, 16], replicated, may hold values from -1.5 to 1.5
- weight_out: bfloat16 [128, 3], replicated, may hold values from -0.5 to 0.5
- bias_out: float32 [3], replicated, may hold values from -3 to 3
Outputs:
- blended: float32 [3, 128, 256, 128], P(None, 'tm', 'rows')
Inputs may be any that keep to these rules, and one draw needn't show every extreme that they name: `frame_slot`: every queue slot holds exactly one frame.
All inputs are finite; a program needn't handle non-finite values.
Results may differ from a plain program's by a relative error of at most 0.0038.
Values may be sent and summed in bfloat16 or wider, within the bound.
No kernel may reach another device: no remote copies, remote signals or barrier semaphores. Data moves between devices by JAX's collectives and lax.ppermute only.
A program may use at most 128 MiB of HBM per device.

v0:
```python
import jax
import jax.numpy as jnp
from jax import lax
from jax.sharding import PartitionSpec as P

UPSCALE = 8


def passed_along(shard, axis, by):
    size = lax.axis_size(axis)
    pairs = [(i, i + by) for i in range(size) if 0 <= i + by < size]
    return lax.ppermute(shard, axis, pairs)


def extended(block, sides, width):
    for axis, dim in sides:
        count = lax.axis_size(axis)
        forward = [(i, i + 1) for i in range(count - 1)]
        backward = [(target, source) for source, target in forward]
        low = lax.ppermute(
            lax.slice_in_dim(block, block.shape[dim] - width, None, axis=dim), axis, forward
        )
        high = lax.ppermute(lax.slice_in_dim(block, 0, width, axis=dim), axis, backward)
        block = jnp.concatenate([low, block, high], axis=dim)
    return block


def conv_rows(source, weight):
    return lax.conv_general_dilated(
        source,
        weight,
        (1, 1),
        ((0, 0), (1, 1)),
        dimension_numbers=("CNHW", "HWIO", "CNHW"),
        preferred_element_type=jnp.float32,
    )


def norm_act(hidden, gain_mid):
    scale = lax.rsqrt(jnp.mean(hidden * hidden, axis=0, keepdims=True) + 1e-06)
    return jax.nn.silu(hidden * scale * gain_mid[:, None, None, None]).astype(jnp.bfloat16)


def predict(spatial, time_mix, weight_out, bias_out):
    mixed = jnp.einsum("cfg,cgrw->cfrw", time_mix, spatial, preferred_element_type=jnp.float32)
    outer = jax.nn.silu(spatial.astype(jnp.float32) + mixed).astype(jnp.bfloat16)
    return (
        jnp.einsum("co,cfrw->ofrw", weight_out, outer, preferred_element_type=jnp.float32)
        + bias_out[:, None, None, None]
    )


def spread(values):
    return values[None, :, None, None]


def body(
    noisy_frames,
    base_queue,
    frame_slot,
    blend_weight,
    weight_in,
    bias_in,
    gain_mid,
    weight_mid,
    time_mix,
    weight_out,
    bias_out,
):
    window = noisy_frames.shape[1]
    half = window // 2
    time_index = lax.axis_index("tm")
    time_count = lax.axis_size("tm")
    ahead = passed_along(noisy_frames[:, :half], "tm", -1)
    noisy_ext = jnp.concatenate([noisy_frames, ahead], axis=1)
    queue_all = lax.all_gather(base_queue, "tm", axis=0, tiled=True)
    total_frames = queue_all.shape[0]
    wanted = jnp.minimum(
        time_index * window + jnp.arange(window + half, dtype=jnp.int32), total_frames - 1
    )
    slots = jnp.take(frame_slot, wanted)
    chosen = jnp.transpose(jnp.take(queue_all, slots, axis=0), (1, 0, 2, 3))
    lifted = jnp.repeat(jnp.repeat(chosen, UPSCALE, axis=2), UPSCALE, axis=3)
    inputs = jnp.concatenate([noisy_ext, lifted], axis=0)
    rimmed = extended(inputs, (("rows", 2),), 1)
    hidden = conv_rows(rimmed, weight_in) + bias_in[:, None, None, None]
    active = norm_act(hidden, gain_mid)
    active_rim = extended(active, (("rows", 2),), 1)
    spatial = conv_rows(active_rim, weight_mid).astype(jnp.bfloat16)
    first_pred = predict(spatial[:, :window], time_mix, weight_out, bias_out)
    second_pred = predict(spatial[:, half:], time_mix, weight_out, bias_out)
    arrived = passed_along(second_pred[:, half:].astype(jnp.bfloat16), "tm", 1).astype(jnp.float32)
    weights = blend_weight.astype(jnp.float32)
    has_prev = (time_index > 0).astype(jnp.float32)
    has_next = (time_index < time_count - 1).astype(jnp.float32)
    lead_early = weights[:half, 0]
    trail_early = weights[:half, 1] * has_prev
    lead_late = weights[half:, 0] * has_next
    trail_late = weights[half:, 1]
    early = (spread(lead_early) * first_pred[:, :half] + spread(trail_early) * arrived) / spread(
        lead_early + trail_early
    )
    late = (
        spread(lead_late) * second_pred[:, :half] + spread(trail_late) * first_pred[:, half:]
    ) / spread(lead_late + trail_late)
    return jnp.concatenate([early, late], axis=1)


def solution(mesh):
    return jax.shard_map(
        body,
        mesh=mesh,
        in_specs=(
            P(None, "tm", "rows", None),
            P("tm", None, "rows", None),
            P(),
            P("tm", None),
            P(),
            P(),
            P(),
            P(),
            P(),
            P(),
            P(),
        ),
        out_specs=P(None, "tm", "rows", None),
        check_vma=False,
    )
```

profile of v0, /device:TPU:95, one launch (start us, length us, event | category | flops | bytes accessed | tf_op | source)
XLA Modules:
  0.0 207.1 jit_solution(14970817570029630332)
XLA Ops:
  0.0 0.8 slice.47
  0.9 2.4 %collective-permute-start = (bf16[3,8,8,128]{3,2,1,0:T(8,128)(2,1)S(1)}, bf16[3,8,8,128]{3,2,1,0:T(8,128)(2,1)S(1)}, u32[]{:S(2)}, u32[]{:S(2)}) collective-permute-start(bf16[3,8,8,128]{3,2,1,0:T(8,128)(2,1)S(1)} %slice.47), channel_id=1, source_target_pairs={{32,0},{64,32},{96,64},{128,96},{160,128},{192,160},{224,192},{33,... | collective-permute-start | bytes 147464 | tf_op jit(solution)/shard_map/ppermute | solution.py:12
  3.3 1.4 gather_fusion
  4.7 22.3 %all_gather.3 = bf16[128,3,1,16]{3,0,2,1:T(8,128)(2,1)S(1)} all-gather(bf16[16,3,1,16]{3,0,2,1:T(8,128)(2,1)} %param.12), channel_id=1, replica_groups=mesh['tm'=8,'rows'=32] {'tm'}, dimensions={0}, use_global_device_ids=true | all-gather | bytes 13824 | tf_op jit(solution)/shard_map/all_gather | solution.py:76
  27.1 0.6 gather_fusion.1
  28.1 0.9 pad_maximum_fusion
  29.3 12.7 %collective-permute-start.1 = (bf16[6,24,1,128]{1,0,3,2:T(8,128)(2,1)S(1)}, bf16[6,24,1,128]{1,0,3,2:T(8,128)(2,1)S(1)}, u32[]{:S(2)}, u32[]{:S(2)}) collective-permute-start(bf16[6,24,1,128]{1,0,3,2:T(8,128)(2,1)S(1)} %copy.127), channel_id=1, source_target_pairs={{0,1},{1,2},{2,3},{3,4},{4,5},{5,6},{6,7},{7,8},{8,9},{9,10},{10,1... | collective-permute-start | bytes 110600 | tf_op jit(solution)/shard_map/ppermute | solution.py:20
  42.2 1.9 collective-permute-start.2
  44.2 1.1 copy.129
  45.3 2.8 %collective-permute-done.1 = bf16[6,24,1,128]{1,0,3,2:T(8,128)(2,1)S(1)} collective-permute-done((bf16[6,24,1,128]{1,0,3,2:T(8,128)(2,1)S(1)}, bf16[6,24,1,128]{1,0,3,2:T(8,128)(2,1)S(1)}, u32[]{:S(2)}, u32[]{:S(2)}) %collective-permute-start.1) | collective-permute-done | bytes 36896 | tf_op jit(solution)/shard_map/ppermute | solution.py:20
  48.0 8.9 %collective-permute-done.2 = bf16[6,24,1,128]{1,0,3,2:T(8,128)(2,1)} collective-permute-done((bf16[6,24,1,128]{1,0,3,2:T(8,128)(2,1)S(1)}, bf16[6,24,1,128]{1,0,3,2:T(8,128)(2,1)}, u32[]{:S(2)}, u32[]{:S(2)}) %collective-permute-start.2) | collective-permute-done | bytes 36896 | tf_op jit(solution)/shard_map/ppermute | solution.py:23
  56.9 11.0 %multiply_reduce_fusion = (f32[24,8,128]{0,2,1:T(8,128)S(1)}, f32[128,24,8,128]{0,1,3,2:T(8,128)}) fusion(f32[128]{0:T(128)} %param.16, bf16[3,3,6,128]{3,2,1,0:T(8,128)(2,1)} %param.15, bf16[6,24,1,128]{1,0,3,2:T(8,128)(2,1)} %collective-permute-done.2, bf16[6,24,8,128]{1,0,3,2:T(8,128)(2,1)S(1)} %copy.129, ...), kind=kOutput, calls=%fused_computation.3 | convolution fusion | flops 348487680 | bytes 13064192 | tf_op jit(solution)/shard_map/conv_general_dilated | solution.py:29
  68.4 6.7 %multiply_convert_fusion = bf16[128,24,8,128]{0,1,3,2:T(8,128)(2,1)S(1)} fusion(f32[128,24,8,128]{0,1,3,2:T(8,128)} %get-tuple-element.24, f32[128]{0:T(128)S(1)} %copy-done.7, f32[24,8,128]{0,2,1:T(8,128)S(1)} %copy.131, f32[128]{0:T(128)S(1)} %copy-done.6), kind=kLoop, calls=%fused_computation.2 | loop fusion | flops 25165824 | bytes 18973696 | tf_op jit(solution)/shard_map/convert_element_type | solution.py:41
  75.1 2.7 %copy-done.3 = bf16[128,24,8,128]{0,1,3,2:T(8,128)(2,1)} copy-done((bf16[128,24,8,128]{0,1,3,2:T(8,128)(2,1)}, bf16[128,24,8,128]{0,1,3,2:T(8,128)(2,1)S(1)}, u32[]{:S(2)}) %copy-start.3) | copy-done | bytes 6291480
  78.1 1.9 collective-permute-start.3
  80.0 2.6 %collective-permute-start.4 = (bf16[128,24,1,128]{0,1,3,2:T(8,128)(2,1)S(1)}, bf16[128,24,1,128]{0,1,3,2:T(8,128)(2,1)}, u32[]{:S(2)}, u32[]{:S(2)}) collective-permute-start(bf16[128,24,1,128]{0,1,3,2:T(8,128)(2,1)S(1)} %get-tuple-element.12), channel_id=1, source_target_pairs={{1,0},{2,1},{3,2},{4,3},{5,4},{6,5},{7,6},{8,7},{9,8},{10,9},{11,1... | collective-permute-start | bytes 2359304 | tf_op jit(solution)/shard_map/ppermute | solution.py:23
  83.1 12.0 %collective-permute-done.3 = bf16[128,24,1,128]{0,1,3,2:T(8,128)(2,1)} collective-permute-done((bf16[128,24,1,128]{0,1,3,2:T(8,128)(2,1)S(1)}, bf16[128,24,1,128]{0,1,3,2:T(8,128)(2,1)}, u32[]{:S(2)}, u32[]{:S(2)}) %collective-permute-start.3) | collective-permute-done | bytes 786464 | tf_op jit(solution)/shard_map/ppermute | solution.py:20
  95.2 7.5 %collective-permute-done.4 = bf16[128,24,1,128]{0,1,3,2:T(8,128)(2,1)} collective-permute-done((bf16[128,24,1,128]{0,1,3,2:T(8,128)(2,1)S(1)}, bf16[128,24,1,128]{0,1,3,2:T(8,128)(2,1)}, u32[]{:S(2)}, u32[]{:S(2)}) %collective-permute-start.4) | collective-permute-done | bytes 786464 | tf_op jit(solution)/shard_map/ppermute | solution.py:23
  102.7 16.9 %fusion.8 = bf16[128,24,8,128]{0,1,3,2:T(8,128)(2,1)S(1)} fusion(bf16[3,3,128,128]{3,2,1,0:T(8,128)(2,1)S(1)} %copy-done, bf16[128,24,1,128]{0,1,3,2:T(8,128)(2,1)} %collective-permute-done.4, bf16[128,24,8,128]{0,1,3,2:T(8,128)(2,1)} %copy-done.3, bf16[128,24,1,128]{0,1,3,2:T(8,128)(2,1)} %collective-permute-done.3), kind=kOutput, calls=%fused_computation.16 | convolution fusion | flops 7236747264 | bytes 14450688 | tf_op jit(solution)/shard_map/conv_general_dilated | solution.py:29
  119.6 4.5 %fusion.34 = (bf16[128,16,8,128]{0,1,3,2:T(8,128)(2,1)}, bf16[128,16,8,128]{0,1,3,2:T(8,128)(2,1)}) fusion(bf16[128,24,8,128]{0,1,3,2:T(8,128)(2,1)S(1)} %fusion.8), kind=kLoop, calls=%fused_computation.65 | loop fusion | bytes 16777216 | tf_op jit(solution)/shard_map/slice | solution.py:91
  124.1 0.9 copy-done.2
  125.0 7.3 %copy.132 = bf16[128,16,8,128]{3,1,2,0:T(8,128)(2,1)} copy(bf16[128,16,8,128]{0,1,3,2:T(8,128)(2,1)} %get-tuple-element.10) | data formatting | bytes 8388608 | tf_op jit(solution)/shard_map/slice | solution.py:90
  132.2 6.7 %fusion.37 = f32[128,8,128,16]{2,3,1,0:T(8,128)} fusion(bf16[128,16,16,1]{2,1,3,0:T(8,128)(2,1)S(1)} %copy.140, bf16[128,16,8,128]{3,1,2,0:T(8,128)(2,1)} %copy.132), kind=kOutput, calls=%fused_computation.68 | convolution fusion | flops 67108864 | bytes 12648448 | tf_op jit(solution)/shard_map/cfg,cgrw->cfrw/dot_general | solution.py:45
  138.9 9.3 %copy.134 = f32[128,8,128,16]{0,3,2,1:T(8,128)} copy(f32[128,8,128,16]{2,3,1,0:T(8,128)} %fusion.37) | data formatting | bytes 16777216 | tf_op jit(solution)/shard_map/cfg,cgrw->cfrw/dot_general | solution.py:45
  148.2 14.4 %fusion.6 = f32[16,8,128,3]{0,3,2,1:T(4,128)S(1)} fusion(f32[128,8,128,16]{0,3,2,1:T(8,128)} %copy.134, bf16[128,3]{0,1:T(4,128)(2,1)S(1)} %copy-done.9, bf16[128,24,8,128]{0,1,3,2:T(8,128)(2,1)} %copy-done.2), kind=kOutput, calls=%fused_computation.14 | convolution fusion | flops 27262976 | bytes 12780288 | tf_op jit(solution)/shard_map/co,cfrw->ofrw/dot_general | solution.py:48
  163.1 7.3 %copy.136 = bf16[128,16,8,128]{3,1,2,0:T(8,128)(2,1)} copy(bf16[128,16,8,128]{0,1,3,2:T(8,128)(2,1)} %get-tuple-element.9) | data formatting | bytes 8388608 | tf_op jit(solution)/shard_map/slice | solution.py:91
  170.4 6.7 %fusion.38 = f32[128,8,128,16]{2,3,1,0:T(8,128)} fusion(bf16[128,16,16,1]{2,1,3,0:T(8,128)(2,1)S(1)} %copy.140, bf16[128,16,8,128]{3,1,2,0:T(8,128)(2,1)} %copy.136), kind=kOutput, calls=%fused_computation.69 | convolution fusion | flops 67108864 | bytes 12648448 | tf_op jit(solution)/shard_map/cfg,cgrw->cfrw/dot_general | solution.py:45
  177.1 9.3 %copy.138 = f32[128,8,128,16]{0,3,2,1:T(8,128)} copy(f32[128,8,128,16]{2,3,1,0:T(8,128)} %fusion.38) | data formatting | bytes 16777216 | tf_op jit(solution)/shard_map/cfg,cgrw->cfrw/dot_general | solution.py:45
  186.4 14.5 %fusion.7 = f32[16,8,128,3]{0,3,2,1:T(4,128)S(1)} fusion(f32[128,8,128,16]{0,3,2,1:T(8,128)} %copy.138, bf16[128,3]{0,1:T(4,128)(2,1)S(1)} %copy-done.9, bf16[128,24,8,128]{0,1,3,2:T(8,128)(2,1)} %copy-done.2), kind=kOutput, calls=%fused_computation.15 | convolution fusion | flops 27262976 | bytes 12780288 | tf_op jit(solution)/shard_map/co,cfrw->ofrw/dot_general | solution.py:48
  201.5 2.4 %collective-permute-start.5 = (bf16[3,8,8,128]{3,2,1,0:T(8,128)(2,1)S(1)}, bf16[3,8,8,128]{3,2,1,0:T(8,128)(2,1)S(1)}, u32[]{:S(2)}, u32[]{:S(2)}) collective-permute-start(bf16[3,8,8,128]{3,2,1,0:T(8,128)(2,1)S(1)} %slice.105), channel_id=1, source_target_pairs={{0,32},{32,64},{64,96},{96,128},{128,160},{160,192},{192,224},{1,3... | collective-permute-start | bytes 147464 | tf_op jit(solution)/shard_map/ppermute | solution.py:12
  204.0 2.3 %collective-permute-done.5 = bf16[3,8,8,128]{3,2,1,0:T(8,128)(2,1)S(1)} collective-permute-done((bf16[3,8,8,128]{3,2,1,0:T(8,128)(2,1)S(1)}, bf16[3,8,8,128]{3,2,1,0:T(8,128)(2,1)S(1)}, u32[]{:S(2)}, u32[]{:S(2)}) %collective-permute-start.5) | collective-permute-done | bytes 49184 | tf_op jit(solution)/shard_map/ppermute | solution.py:12
  206.4 0.7 pad_maximum_fusion.1
  (46 shorter events, 3.5 us)
Async XLA Ops:
  0.0 102.7 %copy-start = (bf16[3,3,128,128]{3,2,1,0:T(8,128)(2,1)S(1)}, bf16[3,3,128,128]{3,2,1,0:T(8,128)(2,1)}, u32[]{:S(2)}) copy-start(bf16[3,3,128,128]{3,2,1,0:T(8,128)(2,1)} %param.18) | copy-start | bytes 884740
  0.9 27.2 %collective-permute-start = (bf16[3,8,8,128]{3,2,1,0:T(8,128)(2,1)S(1)}, bf16[3,8,8,128]{3,2,1,0:T(8,128)(2,1)S(1)}, u32[]{:S(2)}, u32[]{:S(2)}) collective-permute-start(bf16[3,8,8,128]{3,2,1,0:T(8,128)(2,1)S(1)} %slice.47), channel_id=1, source_target_pairs={{32,0},{64,32},{96,64},{128,96},{160,128},{192,160},{224,192},{33,... | collective-permute-start | bytes 147464 | tf_op jit(solution)/shard_map/ppermute | solution.py:12
  29.3 18.7 %collective-permute-start.1 = (bf16[6,24,1,128]{1,0,3,2:T(8,128)(2,1)S(1)}, bf16[6,24,1,128]{1,0,3,2:T(8,128)(2,1)S(1)}, u32[]{:S(2)}, u32[]{:S(2)}) collective-permute-start(bf16[6,24,1,128]{1,0,3,2:T(8,128)(2,1)S(1)} %copy.127), channel_id=1, source_target_pairs={{0,1},{1,2},{2,3},{3,4},{4,5},{5,6},{6,7},{7,8},{8,9},{9,10},{10,1... | collective-permute-start | bytes 110600 | tf_op jit(solution)/shard_map/ppermute | solution.py:20
  42.2 14.7 %collective-permute-start.2 = (bf16[6,24,1,128]{1,0,3,2:T(8,128)(2,1)S(1)}, bf16[6,24,1,128]{1,0,3,2:T(8,128)(2,1)}, u32[]{:S(2)}, u32[]{:S(2)}) collective-permute-start(bf16[6,24,1,128]{1,0,3,2:T(8,128)(2,1)S(1)} %copy.128), channel_id=1, source_target_pairs={{1,0},{2,1},{3,2},{4,3},{5,4},{6,5},{7,6},{8,7},{9,8},{10,9},{11,1... | collective-permute-start | bytes 110600 | tf_op jit(solution)/shard_map/ppermute | solution.py:23
  45.2 23.1 %copy-start.6 = (f32[128]{0:T(128)S(1)}, f32[128]{0:T(128)}, u32[]{:S(2)}) copy-start(f32[128]{0:T(128)} %param.16) | copy-start | bytes 1540
  45.2 23.1 %copy-start.7 = (f32[128]{0:T(128)S(1)}, f32[128]{0:T(128)}, u32[]{:S(2)}) copy-start(f32[128]{0:T(128)} %param.17) | copy-start | bytes 1540
  68.4 14.2 %copy-start.4 = (bf16[128,16,16]{0,2,1:T(8,128)(2,1)S(1)}, bf16[128,16,16]{0,2,1:T(8,128)(2,1)}, u32[]{:S(2)}) copy-start(bf16[128,16,16]{0,2,1:T(8,128)(2,1)} %param.19) | copy-start | bytes 196612
  68.4 14.6 %copy-start.5 = (s32[16,2]{0,1:T(2,128)S(1)}, s32[16,2]{0,1:T(2,128)}, u32[]{:S(2)}) copy-start(s32[16,2]{0,1:T(2,128)} %param.14) | copy-start | bytes 388
  75.1 2.7 %copy-start.3 = (bf16[128,24,8,128]{0,1,3,2:T(8,128)(2,1)}, bf16[128,24,8,128]{0,1,3,2:T(8,128)(2,1)S(1)}, u32[]{:S(2)}) copy-start(bf16[128,24,8,128]{0,1,3,2:T(8,128)(2,1)S(1)} %multiply_convert_fusion) | copy-start | bytes 18874372
  78.1 17.1 %collective-permute-start.3 = (bf16[128,24,1,128]{0,1,3,2:T(8,128)(2,1)S(1)}, bf16[128,24,1,128]{0,1,3,2:T(8,128)(2,1)}, u32[]{:S(2)}, u32[]{:S(2)}) collective-permute-start(bf16[128,24,1,128]{0,1,3,2:T(8,128)(2,1)S(1)} %get-tuple-element.11), channel_id=1, source_target_pairs={{0,1},{1,2},{2,3},{3,4},{4,5},{5,6},{6,7},{7,8},{8,9},{9,10},{10,1... | collective-permute-start | bytes 2359304 | tf_op jit(solution)/shard_map/ppermute | solution.py:20
  80.0 22.7 %collective-permute-start.4 = (bf16[128,24,1,128]{0,1,3,2:T(8,128)(2,1)S(1)}, bf16[128,24,1,128]{0,1,3,2:T(8,128)(2,1)}, u32[]{:S(2)}, u32[]{:S(2)}) collective-permute-start(bf16[128,24,1,128]{0,1,3,2:T(8,128)(2,1)S(1)} %get-tuple-element.12), channel_id=1, source_target_pairs={{1,0},{2,1},{3,2},{4,3},{5,4},{6,5},{7,6},{8,7},{9,8},{10,9},{11,1... | collective-permute-start | bytes 2359304 | tf_op jit(solution)/shard_map/ppermute | solution.py:23
  119.6 5.4 %copy-start.2 = (bf16[128,24,8,128]{0,1,3,2:T(8,128)(2,1)}, bf16[128,24,8,128]{0,1,3,2:T(8,128)(2,1)S(1)}, u32[]{:S(2)}) copy-start(bf16[128,24,8,128]{0,1,3,2:T(8,128)(2,1)S(1)} %fusion.8) | copy-start | bytes 18874372
  138.9 9.3 %copy-start.9 = (bf16[128,3]{0,1:T(4,128)(2,1)S(1)}, bf16[128,3]{0,1:T(4,128)(2,1)}, u32[]{:S(2)}) copy-start(bf16[128,3]{0,1:T(4,128)(2,1)} %param.20) | copy-start | bytes 2308
  186.4 15.0 %copy-start.8 = (f32[3]{0:T(128)S(1)}, f32[3]{0:T(128)}, u32[]{:S(2)}) copy-start(f32[3]{0:T(128)} %param.21) | copy-start | bytes 40
  186.4 20.8 %copy-start.1 = (bf16[3,3,128,128]{3,2,1,0:T(8,128)(2,1)S(1)}, bf16[3,3,128,128]{3,2,1,0:T(8,128)(2,1)}, u32[]{:S(2)}) copy-start(bf16[3,3,128,128]{3,2,1,0:T(8,128)(2,1)} %param.18) | copy-start | bytes 884740
  201.5 4.8 %collective-permute-start.5 = (bf16[3,8,8,128]{3,2,1,0:T(8,128)(2,1)S(1)}, bf16[3,8,8,128]{3,2,1,0:T(8,128)(2,1)S(1)}, u32[]{:S(2)}, u32[]{:S(2)}) collective-permute-start(bf16[3,8,8,128]{3,2,1,0:T(8,128)(2,1)S(1)} %slice.105), channel_id=1, source_target_pairs={{0,32},{32,64},{64,96},{96,128},{128,160},{160,192},{192,224},{1,3... | collective-permute-start | bytes 147464 | tf_op jit(solution)/shard_map/ppermute | solution.py:12
where the time goes:
time: 211 us; the launch traced here: 207 us
  matrix products  70.1 us (33%)
  local copies, waits for them, and re-layouts  48 us (23%)
  waiting for transfers between devices  33.6 us (16%)
  starting transfers between devices  24 us (11%)
  blocking collectives  22.3 us (11%)
  other arithmetic  8.77 us (4%)
    dot_general x2, matrix products, predict(): jnp.einsum('co,cfrw->ofrw', weight_out, outer, preferred_element_type=jnp...  28.9 us
    conv_general_dilated x2, matrix products, conv_rows(): lax.conv_general_dilated(source, weight, (1, 1), ((0, 0), (1, 1)), dimens...  27.9 us
    all_gather x1, blocking collectives, body(): queue_all = lax.all_gather(base_queue, 'tm', axis=0, tiled=True)  22.3 us
    dot_general x2, local copies, waits for them, and re-layouts, predict(): jnp.einsum('cfg,cgrw->cfrw', time_mix, spatial, preferred_element_type=jn...  18.6 us
    ppermute x2, waiting for transfers between devices, extended(): lax.ppermute(lax.slice_in_dim(block, 0, width, axis=dim), axis, backward)  16.4 us
    ppermute x2, waiting for transfers between devices, extended(): lax.ppermute(lax.slice_in_dim(block, block.shape[dim] - width, None, axis...  14.8 us
    ppermute x2, starting transfers between devices, extended(): lax.ppermute(lax.slice_in_dim(block, block.shape[dim] - width, None, axis...  14.6 us
    dot_general x2, matrix products, predict(): jnp.einsum('cfg,cgrw->cfrw', time_mix, spatial, preferred_element_type=jn...  13.3 us
  transfers between devices with their start and end apart: 6, of which 5 were waited for; matrix products, arithmetic and copies ran while one was open for 2% of the time, Pallas kernels for 0%

commit v1 on v0

v1 whole, which is shorter than its diff:
```python
import functools

import jax
import jax.numpy as jnp
import numpy as np
from jax import lax
from jax.experimental import pallas as pl
from jax.experimental.pallas import tpu as pltpu
from jax.sharding import PartitionSpec as P

BF16 = jnp.bfloat16
F32 = jnp.float32
NT = (((1,), (1,)), ((), ()))
VMEM = pl.BlockSpec(memory_space=pltpu.VMEM)
SMEM = pl.BlockSpec(memory_space=pltpu.SMEM)
PARAMS = pltpu.CompilerParams(vmem_limit_bytes=56 * 2**20)


def column_of_pixel():
    p = np.arange(128)
    return (p % 16) * 8 + p // 16


def shift_matrix():
    m = np.zeros((128, 3, 128), np.float32)
    col = column_of_pixel()
    for dv in range(3):
        for p in range(128):
            c = col[p] + dv - 1
            if 0 <= c < 128:
                m[p, dv, c] = 1
    return m.reshape(128, 384)


def unorder_matrix():
    m = np.zeros((128, 128), np.float32)
    m[np.arange(128), column_of_pixel()] = 1
    return m


def widen_matrix():
    m = np.zeros((128, 3, 128), np.float32)
    for br in range(3):
        for c in range(128):
            m[br * 16 + c // 8, br, c] = 1
    return m.reshape(128, 384)


def tap_matrix():
    m = np.zeros((5, 2, 256, 64), np.float32)
    for q in range(5):
        for e in range(2):
            for dr in range(3):
                row = 2 * q + e - 2 + dr
                for dv in range(3):
                    for ch in range(6):
                        tap = (dr * 3 + dv) * 6 + ch
                        if ch < 3:
                            if 0 <= row < 8:
                                k = ch * 8 + row
                            else:
                                k = 24 + ch * 8 + (row + 2 if row < 0 else row - 6)
                            m[q, e, dv * 80 + k, tap] += 1
                        else:
                            br = 0 if row < 0 else (1 if row < 8 else 2)
                            m[q, e, dv * 80 + 48 + br * 8 + ch - 3, tap] += 1
                            m[q, e, dv * 80 + 48 + br * 8 + ch, tap] += 1
    return m.reshape(10, 256, 64)


def iota(shape, dim):
    return lax.broadcasted_iota(jnp.int32, shape, dim)


def prepare_kernel(taps, win, bias, wmid, mix, wout, w_in, w_mid, w_mix, w_out):
    k = iota((256, 128), 0)
    low = (k % 80 >= 48) & (k % 80 < 72) & (k % 8 >= 3) & (k % 8 < 6) & (k < 240)
    b = bias[...]
    b0 = b.astype(BF16).astype(F32)
    b1 = (b - b0).astype(BF16).astype(F32)
    b2 = b - b0 - b1
    for q in range(5):
        for e in range(2):
            v = jnp.dot(taps[2 * q + e], win[...], preferred_element_type=F32)
            v = jnp.where(low, v - v.astype(BF16).astype(F32), v)
            v = jnp.where(k == 152, b0, jnp.where(k == 153, b1, jnp.where(k == 154, b2, v)))
            w_in[q, :, e * 128 : (e + 1) * 128] = v.astype(BF16)
    w_mid[...] = jnp.zeros_like(w_mid)
    for dr in range(3):
        for dv in range(3):
            t = wmid[dr * 3 + dv].T
            for e in range(2):
                tap = (dr + e) * 3 + dv
                w_mid[e * 128 : (e + 1) * 128, tap * 128 : (tap + 1) * 128] = t
    r = iota((256, 256), 0)
    c = iota((256, 256), 1)
    reorder = ((r // 16 == c % 16) & (r % 16 == c // 16)).astype(BF16)
    over = (iota((16, 256), 0) == iota((16, 256), 1) // 16).astype(BF16)
    same = r % 16 == c % 16
    for g in range(8):
        t = jnp.dot(reorder, mix[g * 256 : (g + 1) * 256, :], preferred_element_type=F32)
        t = jnp.dot(t.astype(BF16), over, preferred_element_type=F32)
        w_mix[g] = jnp.where(same, t, 0.0).astype(BF16)
    own = iota((16, 256), 0) == iota((16, 256), 1) // 16
    for g in range(8):
        pick = (iota((128, 256), 0) == g * 16 + iota((128, 256), 1) % 16).astype(BF16)
        t = jnp.dot(wout[...], pick, preferred_element_type=F32)
        for o in range(3):
            w_out[g, o * 16 : (o + 1) * 16, :] = jnp.where(own, t[o : o + 1, :], 0.0).astype(BF16)


def lift(base, hot, widen, lifted):
    chosen = jnp.dot(hot[...], base[...], preferred_element_type=F32).astype(BF16)
    lifted[...] = jnp.dot(chosen, widen[...], preferred_element_type=F32)


def activate(own, rim, first, lifted, lift_first, shift, w_in, mean, gain, depth, act):
    ones = jnp.ones((8, 128), F32)
    zero = jnp.zeros((80, 128), BF16)
    end = jnp.zeros((16, 384), BF16)
    for f in range(8):
        tiles = [own[ch, first + f].astype(F32) for ch in range(3)]
        tiles += [rim[ch, first + f].astype(F32) for ch in range(3)]
        at = (lift_first + f) * 8
        tiles += [lifted[at : at + 8, br * 128 : (br + 1) * 128] for br in range(3)]
        x = jnp.concatenate(tiles + [ones], axis=0).astype(BF16)
        x = jnp.concatenate(
            [
                jnp.concatenate([x, zero, zero], axis=1),
                jnp.concatenate([zero, x, zero], axis=1),
                jnp.concatenate([zero, zero, x], axis=1),
                end,
            ],
            axis=0,
        )
        d = lax.dot_general(shift[...], x, NT, preferred_element_type=F32)
        depth[f * 128 : (f + 1) * 128, :] = d.astype(BF16)
    s = iota((16, 256), 0)
    for q in range(5):
        h = jnp.dot(depth[...], w_in[q], preferred_element_type=F32)
        ss = jnp.dot((h * h).astype(BF16), mean[...], preferred_element_type=F32)
        u = h * lax.rsqrt(ss + 1e-6) * gain[q : q + 1, :]
        a = (u * jnp.tanh(u) + u).reshape(8, 128, 256)
        body = a.astype(BF16).reshape(8, 8, 16, 256)
        for e in range(2):
            act[:, 2 * q + e, 1:9] = body[:, :, :, e * 128 : (e + 1) * 128]
        for f in range(8):
            left = jnp.where(s == 0, 0.0, pltpu.roll(a[f, 112:128], 1, 0)).astype(BF16)
            right = jnp.where(s == 15, 0.0, pltpu.roll(a[f, 0:16], 15, 0)).astype(BF16)
            for e in range(2):
                act[f, 2 * q + e, 0] = left[:, e * 128 : (e + 1) * 128]
                act[f, 2 * q + e, 9] = right[:, e * 128 : (e + 1) * 128]


def convolve(act, w_mid, spatial, first):
    @pl.loop(0, 4)
    def _(pair):
        for i in range(4):
            frames = []
            for b in range(2):
                taps = [
                    act[pair * 2 + b, 2 * i + dr, dv : dv + 8].reshape(128, 128)
                    for dr in range(4)
                    for dv in range(3)
                ]
                frames.append(jnp.concatenate(taps, axis=1))
            x = jnp.concatenate(frames, axis=0)
            y = lax.dot_general(w_mid[...], x, NT, preferred_element_type=F32).astype(BF16)
            for b in range(2):
                for e in range(2):
                    spatial[i, first + pair * 2 + b, :, e * 128 : (e + 1) * 128] = y[
                        e * 128 : (e + 1) * 128, b * 128 : (b + 1) * 128
                    ]


def predict(spatial, w_mix, w_out, bias_out, total):
    @pl.loop(0, 4)
    def _(i):
        acc = None
        for g in range(8):
            x = spatial[i, :, g * 16 : (g + 1) * 16, :].reshape(256, 256)
            h = 0.5 * (jnp.dot(w_mix[g], x, preferred_element_type=F32) + x.astype(F32))
            outer = (h * jnp.tanh(h) + h).astype(BF16)
            p = jnp.dot(w_out[g], outer, preferred_element_type=F32)
            acc = p if acc is None else acc + p
        for o in range(3):
            part = acc[o * 16 : (o + 1) * 16, :] + bias_out[0, o]
            for e in range(2):
                total[2 * i + e, o * 16 : (o + 1) * 16, :] = part[:, e * 128 : (e + 1) * 128]


def unorder(total, order, rows):
    x = total[...].reshape(384, 128)
    x0 = x.astype(BF16)
    r = x - x0.astype(F32)
    x1 = r.astype(BF16)
    x2 = (r - x1.astype(F32)).astype(BF16)
    y = [jnp.dot(part, order[...], preferred_element_type=F32) for part in (x0, x1, x2)]
    rows[...] = y[0] + (y[1] + y[2])


def picture(rows, o, f):
    return rows[pl.ds(o * 16 + f, 8, stride=48), :]


def late_kernel(
    own, ahead, rim, rim_ahead, base, hot, widen, shift, w_in, w_mid, w_mix, w_out, mean, order,
    gain, bias_out, send, near, kept, lifted, depth, act, spatial, total, rows,
):
    lift(base, hot, widen, lifted)
    activate(own, rim, 8, lifted, 0, shift, w_in, mean, gain, depth, act)
    convolve(act, w_mid, spatial, 0)
    activate(ahead, rim_ahead, 0, lifted, 8, shift, w_in, mean, gain, depth, act)
    convolve(act, w_mid, spatial, 8)
    kept[...] = spatial[:, 0:8]
    predict(spatial, w_mix, w_out, bias_out, total)
    unorder(total, order, rows)
    for o in range(3):
        for f in range(8):
            near[o, f] = picture(rows, o, f)
            send[o, f] = picture(rows, o, f + 8).astype(BF16)


def early_kernel(
    own, rim, base, hot, widen, shift, w_in, w_mid, w_mix, w_out, mean, order,
    gain, bias_out, near, kept, share, out, lifted, depth, act, spatial, total, rows,
):
    lift(base, hot, widen, lifted)
    activate(own, rim, 0, lifted, 0, shift, w_in, mean, gain, depth, act)
    spatial[:, 8:16] = kept[...]
    convolve(act, w_mid, spatial, 0)
    predict(spatial, w_mix, w_out, bias_out, total)
    unorder(total, order, rows)
    for o in range(3):
        for f in range(8):
            out[o, f] = picture(rows, o, f) * share[0, f]
            out[o, f + 8] = picture(rows, o, f + 8) * share[1, f + 8] + near[o, f] * share[0, f + 8]


def scratch(frames):
    return [
        pltpu.VMEM((frames * 8, 384), F32),
        pltpu.VMEM((1024, 256), BF16),
        pltpu.VMEM((8, 10, 10, 16, 128), BF16),
        pltpu.VMEM((4, 16, 128, 256), BF16),
        pltpu.VMEM((8, 48, 128), F32),
        pltpu.VMEM((384, 128), F32),
    ]


def shape(dims, kind):
    return jax.ShapeDtypeStruct(dims, kind)


def prepare(weight_in, bias_in, weight_mid, time_mix, weight_out):
    win = jnp.pad(weight_in.reshape(54, 128), ((0, 10), (0, 0)))
    wout = jnp.pad(weight_out.T, ((0, 13), (0, 0)))
    return pl.pallas_call(
        prepare_kernel,
        out_shape=(
            shape((5, 256, 256), BF16),
            shape((256, 1536), BF16),
            shape((8, 256, 256), BF16),
            shape((8, 48, 256), BF16),
        ),
        in_specs=[VMEM] * 6,
        out_specs=(VMEM,) * 4,
        compiler_params=PARAMS,
        cost_estimate=pl.CostEstimate(flops=10**9, bytes_accessed=3 * 10**6, transcendentals=0),
        name="prepare",
    )(
        jnp.asarray(tap_matrix(), BF16),
        win,
        bias_in.reshape(1, 128),
        weight_mid.reshape(9, 128, 128),
        time_mix.reshape(2048, 16),
        wout,
    )


def body(
    noisy_frames, base_queue, frame_slot, blend_weight, weight_in, bias_in, gain_mid, weight_mid,
    time_mix, weight_out, bias_out,
):
    t = lax.axis_index("tm")
    r = lax.axis_index("rows")
    n_t = lax.axis_size("tm")
    n_r = lax.axis_size("rows")
    down = [(i, i + 1) for i in range(n_r - 1)]
    up = [(i + 1, i) for i in range(n_r - 1)]
    back = [(i + 1, i) for i in range(n_t - 1)]
    forth = [(i, i + 1) for i in range(n_t - 1)]

    base = jnp.transpose(base_queue[:, :, 0, :], (1, 0, 2))
    wide = jnp.pad(base, ((0, 0), (0, 0), (0, 112)))[:, :, None, :]
    ahead = lax.ppermute(noisy_frames[:, :8], "tm", back)
    low = lax.ppermute(jnp.concatenate([noisy_frames[:, :, 6:], wide], axis=2), "rows", down)
    high = lax.ppermute(jnp.concatenate([noisy_frames[:, :, :2], wide], axis=2), "rows", up)
    rim = jnp.concatenate(
        [low[:, :, :2], high[:, :, :2], jnp.zeros((3, 16, 4, 128), BF16)], axis=2
    )
    rim_ahead = lax.ppermute(rim[:, :8], "tm", back)
    three = jnp.concatenate([low[:, :, 2, :16], base, high[:, :, 2, :16]], axis=2)
    three = jnp.pad(three.reshape(48, 48), ((0, 0), (0, 80)))
    queue = lax.all_to_all(
        jnp.broadcast_to(three[None], (n_t, 48, 128)), "tm", 0, 0, tiled=True
    ).reshape(384, 128)

    slots = jnp.take(frame_slot, jnp.minimum(t * 16 + jnp.arange(24), 127))
    j = jnp.arange(8)
    place = (slots[:, None] // 16) * 48 + (j[None, :] % 3) * 16 + slots[:, None] % 16
    place = jnp.where(j[None, :] < 6, place, -1).reshape(192, 1)
    hot = (place == jnp.arange(384)[None, :]).astype(BF16)

    w_in, w_mid, w_mix, w_out = prepare(weight_in, bias_in, weight_mid, time_mix, weight_out)
    half_gain = jnp.tile(0.5 * gain_mid, 10).reshape(10, 128)
    inside = jnp.ones((10,), F32).at[0].set((r > 0).astype(F32)).at[9].set((r < n_r - 1).astype(F32))
    gain = (half_gain * inside[:, None]).reshape(5, 256)
    mean = jnp.asarray(np.kron(np.eye(2), np.full((128, 128), 1 / 128)), BF16)
    order = jnp.asarray(unorder_matrix(), BF16)
    shift = jnp.asarray(shift_matrix(), BF16)
    widen = jnp.asarray(widen_matrix(), BF16)
    b_out = bias_out.reshape(1, 3)

    w = blend_weight.astype(F32)
    late = jnp.arange(16) >= 8
    lead = w[:, 0] * jnp.where(late, (t < n_t - 1).astype(F32), 1.0)
    trail = w[:, 1] * jnp.where(late, 1.0, (t > 0).astype(F32))
    share = jnp.stack([lead, trail]) / (lead + trail)[None]
    wide_share = jnp.broadcast_to(share[:, :, None, None], (2, 16, 1, 128))

    send, near, kept = pl.pallas_call(
        late_kernel,
        out_shape=(
            shape((3, 8, 8, 128), BF16),
            shape((3, 8, 8, 128), F32),
            shape((4, 8, 128, 256), BF16),
        ),
        in_specs=[VMEM] * 15 + [SMEM],
        out_specs=(VMEM,) * 3,
        scratch_shapes=scratch(16),
        compiler_params=PARAMS,
        cost_estimate=pl.CostEstimate(flops=10**10, bytes_accessed=10**7, transcendentals=0),
        name="late",
    )(
        noisy_frames, ahead, rim, rim_ahead, queue, hot[64:], widen, shift, w_in, w_mid, w_mix,
        w_out, mean, order, gain, b_out,
    )
    arrived = lax.ppermute(send, "tm", forth)
    mine = pl.pallas_call(
        early_kernel,
        out_shape=shape((3, 16, 8, 128), F32),
        in_specs=[VMEM] * 13 + [SMEM] + [VMEM] * 3,
        out_specs=VMEM,
        scratch_shapes=scratch(8),
        compiler_params=PARAMS,
        cost_estimate=pl.CostEstimate(flops=10**10, bytes_accessed=10**7, transcendentals=0),
        name="early",
    )(
        noisy_frames, rim, queue, hot[:64], widen, shift, w_in, w_mid, w_mix, w_out, mean, order,
        gain, b_out, near, kept, wide_share,
    )
    early = mine[:, :8] + share[1, None, :8, None, None] * arrived.astype(F32)
    return jnp.concatenate([early, mine[:, 8:]], axis=1)


def solution(mesh):
    return jax.shard_map(
        body,
        mesh=mesh,
        in_specs=(
            P(None, "tm", "rows", None),
            P("tm", None, "rows", None),
            P(),
            P("tm", None),
            P(),
            P(),
            P(),
            P(),
            P(),
            P(),
            P(),
        ),
        out_specs=P(None, "tm", "rows", None),
        check_vma=False,
    )
```

time: 211 us -> 81.7 us (0.39); the launches traced: 207 us -> 81 us
  matrix products: 70.1 us -> 0 us
  Pallas kernels: 0 us -> 39.5 us
  local copies, waits for them, and re-layouts: 48 us -> 12.7 us
  waiting for transfers between devices: 33.6 us -> 0.72 us
  blocking collectives: 22.3 us -> 0 us
  other arithmetic: 8.77 us -> 3.42 us
    dot_general x4 -> x0, matrix products: 42.2 us -> none  [the longest x2 28.9 us: predict(): jnp.einsum('co,cfrw->ofrw', weight_out, outer, preferred_element_type=jnp...]
    pallas_call x0 -> x3, Pallas kernels: none -> 39.5 us  [the longest x1 21.2 us: body(): pl.pallas_call(late_kernel, out_shape=(shape((3, 8, 8, 128), BF16), shape...]
    ppermute x6 -> x5, waiting for transfers between devices: 33.6 us -> 0.72 us  [the longest x1 0.71 us: body(): rim_ahead = lax.ppermute(rim[:, :8], 'tm', back)]
    conv_general_dilated x2 -> x0, matrix products: 27.9 us -> none  [conv_rows(): lax.conv_general_dilated(source, weight, (1, 1), ((0, 0), (1, 1)), dimens...]
    all_gather x1 -> x0, blocking collectives: 22.3 us -> none  [body(): queue_all = lax.all_gather(base_queue, 'tm', axis=0, tiled=True)]
    dot_general x4 -> x0, local copies, waits for them, and re-layouts: 19.6 us -> none  [the longest x2 18.6 us: predict(): jnp.einsum('cfg,cgrw->cfrw', time_mix, spatial, preferred_element_type=jn...]
    slice x9, local copies, waits for them, and re-layouts: 20.6 us -> 3.18 us  [the longest x1 1.01 us: body(): noisy_frames[:, :, 6:]]
    convert_element_type x2, other arithmetic: 6.69 us -> 0.78 us  [the longest x1 0.68 us: body(): w = blend_weight.astype(F32)]
  transfers between devices with their start and end apart: 6 -> 6, of which waited for: 5 -> 1; matrix products, arithmetic and copies ran while one was open for 2% -> 15% of each run, Pallas kernels for 0% -> 23%
where the time goes in v1:
time: 81.7 us; the launch traced here: 81 us
  Pallas kernels  39.5 us (48%)
  starting transfers between devices  24.4 us (30%)
  local copies, waits for them, and re-layouts  12.7 us (16%)
  other arithmetic  3.42 us (4%)
    pallas_call x1, Pallas kernels, body(): pl.pallas_call(late_kernel, out_shape=(shape((3, 8, 8, 128), BF16), shape...  21.2 us
    pallas_call x1, Pallas kernels, body(): pl.pallas_call(early_kernel, out_shape=shape((3, 16, 8, 128), F32), in_sp...  14.6 us
    ppermute x1, starting transfers between devices, body(): lax.ppermute(jnp.concatenate([noisy_frames[:, :, 6:], wide], axis=2), 'ro...  7.2 us
    all_to_all x1, starting transfers between devices, body(): lax.all_to_all(jnp.broadcast_to(three[None], (n_t, 48, 128)), 'tm', 0, 0,...  5.3 us
    ppermute x1, starting transfers between devices, body(): arrived = lax.ppermute(send, 'tm', forth)  4.39 us
    pallas_call x1, Pallas kernels, prepare(): pl.pallas_call(prepare_kernel, out_shape=(shape((5, 256, 256), BF16), sha...  3.73 us
    unnamed x19, local copies, waits for them, and re-layouts  3.54 us
    ppermute x1, starting transfers between devices, body(): lax.ppermute(jnp.concatenate([noisy_frames[:, :, :2], wide], axis=2), 'ro...  2.58 us
  transfers between devices with their start and end apart: 6, of which 1 were waited for; matrix products, arithmetic and copies ran while one was open for 15% of the time, Pallas kernels for 23%

profile of v1, /device:TPU:95, one launch (start us, length us, event | category | flops | bytes accessed | tf_op | source)
XLA Modules:
  0.0 81.0 jit_solution(4241839025449199335)
XLA Ops:
  0.0 0.7 pad_bitcast_fusion
  0.8 1.0 %fusion.9 = (bf16[3,16,2,128]{3,2,1,0:T(2,128)(2,1)S(1)}, bf16[3,16,2,128]{3,2,1,0:T(2,128)(2,1)S(1)}) fusion(bf16[3,16,8,128]{3,2,1,0:T(8,128)(2,1)} %own.3), kind=kLoop, calls=%fused_computation.42 | loop fusion | bytes 98304 | tf_op jit(solution)/shard_map/slice | solution.py:297
  1.8 0.1 pad_maximum_fusion.2
  1.9 2.6 %collective-permute-start.1 = (bf16[3,16,3,128]{3,2,1,0:T(4,128)(2,1)S(1)}, bf16[3,16,3,128]{3,2,1,0:T(4,128)(2,1)S(1)}, u32[]{:S(2)}, u32[]{:S(2)}) collective-permute-start(bf16[3,16,3,128]{3,2,1,0:T(4,128)(2,1)S(1)} %get-tuple-element.50), channel_id=1, source_target_pairs={{1,0},{2,1},{3,2},{4,3},{5,4},{6,5},{7,6},{8,7},{9,8},{10,9},{11,1... | collective-permute-start | bytes 110600 | tf_op jit(solution)/shard_map/ppermute | solution.py:298
  4.5 7.2 %collective-permute-start = (bf16[3,16,3,128]{3,2,1,0:T(4,128)(2,1)S(1)}, bf16[3,16,3,128]{3,2,1,0:T(4,128)(2,1)S(1)}, u32[]{:S(2)}, u32[]{:S(2)}) collective-permute-start(bf16[3,16,3,128]{3,2,1,0:T(4,128)(2,1)S(1)} %get-tuple-element.49), channel_id=1, source_target_pairs={{0,1},{1,2},{2,3},{3,4},{4,5},{5,6},{6,7},{7,8},{8,9},{9,10},{10,1... | collective-permute-start | bytes 110600 | tf_op jit(solution)/shard_map/ppermute | solution.py:297
  11.7 0.8 slice.71
  12.5 2.4 %collective-permute-start.2 = (bf16[3,8,8,128]{3,2,1,0:T(8,128)(2,1)S(1)}, bf16[3,8,8,128]{3,2,1,0:T(8,128)(2,1)S(1)}, u32[]{:S(2)}, u32[]{:S(2)}) collective-permute-start(bf16[3,8,8,128]{3,2,1,0:T(8,128)(2,1)S(1)} %slice.71), channel_id=1, source_target_pairs={{32,0},{64,32},{96,64},{128,96},{160,128},{192,160},{224,192},{33,... | collective-permute-start | bytes 147464 | tf_op jit(solution)/shard_map/ppermute | solution.py:296
  15.0 0.7 convert_element_type.26
  15.7 0.7 gather_fusion
  16.6 0.1 fusion
  16.9 0.7 broadcast_multiply_fusion
  17.6 0.6 bitcast_multiply_fusion.gain
  18.2 0.6 slice.85.hot
  18.8 0.6 slice.87.hot
  19.5 0.8 copy.22
  20.2 0.7 reshape.302
  21.0 2.0 %copy.24 = bf16[128,16,16]{2,1,0:T(8,128)(2,1)} copy(bf16[128,16,16]{0,2,1:T(8,128)(2,1)} %param.28) | data formatting | bytes 131072 | tf_op args[8]
  23.0 0.6 pad.24.win
  23.6 0.6 pad.25.wout
  24.7 0.7 broadcast_in_dim.61
  25.3 5.3 %all-to-all-start = ((bf16[8,48,128]{2,1,0:T(8,128)(2,1)}), bf16[8,48,128]{2,1,0:T(8,128)(2,1)S(1)}, u32[]{:S(2)}, u32[]{:S(2)}) async-start(bf16[8,48,128]{2,1,0:T(8,128)(2,1)} %broadcast_in_dim.61), calls=%async_computation | async-start | bytes 196608 | tf_op jit(solution)/shard_map/all_to_all | solution.py:305
  30.7 0.1 maximum_maximum_fusion.rim
  30.8 2.5 %collective-permute-start.3 = (bf16[3,8,8,128]{3,2,1,0:T(8,128)(2,1)S(1)}, bf16[3,8,8,128]{3,2,1,0:T(8,128)(2,1)S(1)}, u32[]{:S(2)}, u32[]{:S(2)}) collective-permute-start(bf16[3,8,8,128]{3,2,1,0:T(8,128)(2,1)S(1)} %slice.86), channel_id=1, source_target_pairs={{32,0},{64,32},{96,64},{128,96},{160,128},{192,160},{224,192},{33,... | collective-permute-start | bytes 147464 | tf_op jit(solution)/shard_map/ppermute | solution.py:302
  33.3 3.7 %prepare.1 = (bf16[5,256,256]{2,1,0:T(8,128)(2,1)}, bf16[256,1536]{1,0:T(8,128)(2,1)}, bf16[8,256,256]{2,1,0:T(8,128)(2,1)}, bf16[8,48,256]{2,1,0:T(8,128)(2,1)}) custom-call(bf16[10,256,64]{2,1,0:T(8,128)(2,1)} %constant.144.clone.taps, bf16[64,128]{1,0:T(8,128)(2,1)} %pad.24.win, f32[1,128]{1,0:T(1,128)} %bitcast.44, bf16[9,128,128]{2,1,0:T(8,128)(2,1)} %bitcast.43, ...), custom_call_target="tpu_custom_call" | custom-call | flops 1000000000 | bytes 3000000 | tf_op jit(solution)/shard_map/prepare/pallas_call | solution.py:258
  37.0 0.7 collective-permute-done.3.rim_ahead
  37.8 0.6 copy-done.6
  38.4 21.2 %late.1 = (bf16[3,8,8,128]{3,2,1,0:T(8,128)(2,1)}, f32[3,8,8,128]{3,2,1,0:T(8,128)}, bf16[4,8,128,256]{3,2,1,0:T(8,128)(2,1)}) custom-call(bf16[3,16,8,128]{3,2,1,0:T(8,128)(2,1)} %own.3, bf16[3,8,8,128]{3,2,1,0:T(8,128)(2,1)} %copy-done.5, bf16[3,16,8,128]{3,2,1,0:T(8,128)(2,1)} %copy-done.1, bf16[3,8,8,128]{3,2,1,0:T(8,128)(2,1)} %copy-done.6, ...), custom_call_target="tpu_custom_call" | custom-call | flops 10000000000 | bytes 10000000 | tf_op jit(solution)/shard_map/late/pallas_call | solution.py:332
  59.6 4.4 %collective-permute-start.4 = (bf16[3,8,8,128]{3,2,1,0:T(8,128)(2,1)}, bf16[3,8,8,128]{3,2,1,0:T(8,128)(2,1)S(1)}, u32[]{:S(2)}, u32[]{:S(2)}) collective-permute-start(bf16[3,8,8,128]{3,2,1,0:T(8,128)(2,1)} %get-tuple-element.42), channel_id=1, source_target_pairs={{0,32},{32,64},{64,96},{96,128},{128,160},{160,192},{192,224},{1,3... | collective-permute-start | bytes 147464 | tf_op jit(solution)/shard_map/ppermute | solution.py:349
  64.0 0.7 broadcast_in_dim.70.share
  64.7 14.6 %early.1 = f32[3,16,8,128]{3,2,1,0:T(8,128)} custom-call(bf16[3,16,8,128]{3,2,1,0:T(8,128)(2,1)} %own.3, bf16[3,16,8,128]{3,2,1,0:T(8,128)(2,1)} %copy-done.1, bf16[384,128]{1,0:T(8,128)(2,1)} %bitcast.37, bf16[64,384]{1,0:T(8,128)(2,1)} %slice.85.hot, bf16[128,384]{1,0:T(8,128)(2,1)} %constant.148.clone.widen, bf16[128,384]{1,0:T(8,128)(2,1)} %constant.147.clone.shift, ...), custom_call_target="tpu_custom_call" | custom-call | flops 10000000000 | bytes 10000000 | tf_op jit(solution)/shard_map/early/pallas_call | solution.py:350
  79.3 1.0 %slice_add_fusion = (f32[3,16,8,128]{3,2,1,0:T(8,128)S(1)}, f32[3,16,8,128]{3,2,1,0:T(8,128)S(1)}) fusion(f32[3,16,8,128]{3,2,1,0:T(8,128)} %early.1, bf16[3,8,8,128]{3,2,1,0:T(8,128)(2,1)S(1)} %collective-permute-done.4, f32[8]{0:T(128)S(1)} %slice_bitcast_fusion, f32[3,16,8,128]{3,2,1,0:T(8,128)S(1)} %custom-call.2), kind=kLoop, output_to_operand_aliasing={{0}: (3, {}), {1}: (3, {})}, calls=%fused_computation.4 | loop fusion | flops 73728 | bytes 442880 | tf_op jit(solution)/shard_map/add | solution.py:363
  80.4 0.7 copy-done.4
  (50 shorter events, 1.0 us)
Async XLA Ops:
  0.0 15.7 %copy-start = (s32[128]{0:T(128)S(1)}, s32[128]{0:T(128)}, u32[]{:S(2)}) copy-start(s32[128]{0:T(128)} %param.22) | copy-start | bytes 1540
  0.0 23.6 %copy-start.3 = (bf16[128,3]{0,1:T(4,128)(2,1)S(1)}, bf16[128,3]{0,1:T(4,128)(2,1)}, u32[]{:S(2)}) copy-start(bf16[128,3]{0,1:T(4,128)(2,1)} %param.29) | copy-start | bytes 2308
  1.9 22.4 %collective-permute-start.1 = (bf16[3,16,3,128]{3,2,1,0:T(4,128)(2,1)S(1)}, bf16[3,16,3,128]{3,2,1,0:T(4,128)(2,1)S(1)}, u32[]{:S(2)}, u32[]{:S(2)}) collective-permute-start(bf16[3,16,3,128]{3,2,1,0:T(4,128)(2,1)S(1)} %get-tuple-element.50), channel_id=1, source_target_pairs={{1,0},{2,1},{3,2},{4,3},{5,4},{6,5},{7,6},{8,7},{9,8},{10,9},{11,1... | collective-permute-start | bytes 110600 | tf_op jit(solution)/shard_map/ppermute | solution.py:298
  4.5 20.0 %collective-permute-start = (bf16[3,16,3,128]{3,2,1,0:T(4,128)(2,1)S(1)}, bf16[3,16,3,128]{3,2,1,0:T(4,128)(2,1)S(1)}, u32[]{:S(2)}, u32[]{:S(2)}) collective-permute-start(bf16[3,16,3,128]{3,2,1,0:T(4,128)(2,1)S(1)} %get-tuple-element.49), channel_id=1, source_target_pairs={{0,1},{1,2},{2,3},{3,4},{4,5},{5,6},{6,7},{7,8},{8,9},{9,10},{10,1... | collective-permute-start | bytes 110600 | tf_op jit(solution)/shard_map/ppermute | solution.py:297
  12.5 24.6 %collective-permute-start.2 = (bf16[3,8,8,128]{3,2,1,0:T(8,128)(2,1)S(1)}, bf16[3,8,8,128]{3,2,1,0:T(8,128)(2,1)S(1)}, u32[]{:S(2)}, u32[]{:S(2)}) collective-permute-start(bf16[3,8,8,128]{3,2,1,0:T(8,128)(2,1)S(1)} %slice.71), channel_id=1, source_target_pairs={{32,0},{64,32},{96,64},{128,96},{160,128},{192,160},{224,192},{33,... | collective-permute-start | bytes 147464 | tf_op jit(solution)/shard_map/ppermute | solution.py:296
  25.3 12.4 %all-to-all-start = ((bf16[8,48,128]{2,1,0:T(8,128)(2,1)}), bf16[8,48,128]{2,1,0:T(8,128)(2,1)S(1)}, u32[]{:S(2)}, u32[]{:S(2)}) async-start(bf16[8,48,128]{2,1,0:T(8,128)(2,1)} %broadcast_in_dim.61), calls=%async_computation | async-start | bytes 196608 | tf_op jit(solution)/shard_map/all_to_all | solution.py:305
  30.8 7.0 %copy-start.1 = (bf16[3,16,8,128]{3,2,1,0:T(8,128)(2,1)}, bf16[3,16,8,128]{3,2,1,0:T(8,128)(2,1)S(1)}, u32[]{:S(2)}) copy-start(bf16[3,16,8,128]{3,2,1,0:T(8,128)(2,1)S(1)} %maximum_maximum_fusion.rim) | copy-start | bytes 294916
  30.8 6.9 %collective-permute-start.3 = (bf16[3,8,8,128]{3,2,1,0:T(8,128)(2,1)S(1)}, bf16[3,8,8,128]{3,2,1,0:T(8,128)(2,1)S(1)}, u32[]{:S(2)}, u32[]{:S(2)}) collective-permute-start(bf16[3,8,8,128]{3,2,1,0:T(8,128)(2,1)S(1)} %slice.86), channel_id=1, source_target_pairs={{32,0},{64,32},{96,64},{128,96},{160,128},{192,160},{224,192},{33,... | collective-permute-start | bytes 147464 | tf_op jit(solution)/shard_map/ppermute | solution.py:302
  37.0 0.7 copy-start.5
  37.7 0.6 copy-start.6
  37.8 0.7 copy-start.2
  59.6 19.7 %collective-permute-start.4 = (bf16[3,8,8,128]{3,2,1,0:T(8,128)(2,1)}, bf16[3,8,8,128]{3,2,1,0:T(8,128)(2,1)S(1)}, u32[]{:S(2)}, u32[]{:S(2)}) collective-permute-start(bf16[3,8,8,128]{3,2,1,0:T(8,128)(2,1)} %get-tuple-element.42), channel_id=1, source_target_pairs={{0,32},{32,64},{64,96},{96,128},{128,160},{160,192},{192,224},{1,3... | collective-permute-start | bytes 147464 | tf_op jit(solution)/shard_map/ppermute | solution.py:349
  80.3 0.7 copy-start.4

commit v2 on v0

v2 whole, which is shorter than its diff:
```python
import functools

import jax
import jax.numpy as jnp
import numpy as np
from jax import lax
from jax.experimental import pallas as pl
from jax.experimental.pallas import tpu as pltpu
from jax.sharding import PartitionSpec as P

BF16 = jnp.bfloat16
F32 = jnp.float32
NT = (((1,), (1,)), ((), ()))
VMEM = pl.BlockSpec(memory_space=pltpu.VMEM)
HBM = pl.BlockSpec(memory_space=pltpu.HBM)
SMEM = pl.BlockSpec(memory_space=pltpu.SMEM)
PARAMS = pltpu.CompilerParams(vmem_limit_bytes=24 * 2**20)


def tap_matrix():
    m = np.zeros((5, 2, 256, 72), np.float32)
    for q in range(5):
        for e in range(2):
            for dr in range(3):
                row = 2 * q + e - 2 + dr
                for dv in range(3):
                    for ch in range(6):
                        tap = (dr * 3 + dv) * 8 + ch
                        if ch < 3:
                            if 0 <= row < 8:
                                k = ch * 8 + row
                            else:
                                k = 24 + ch * 8 + (row + 2 if row < 0 else row - 6)
                            m[q, e, dv * 80 + k, tap] += 1
                        else:
                            br = 0 if row < 0 else (1 if row < 8 else 2)
                            m[q, e, dv * 80 + 48 + br * 8 + ch - 3, tap] += 1
                            m[q, e, dv * 80 + 48 + br * 8 + ch, tap] += 1
    return m.reshape(10, 256, 72)


def spread_matrix():
    m = np.zeros((496, 256), np.float32)
    m[240 + np.arange(256) // 16, np.arange(256)] = 1
    return m


def iota(shape, dim):
    return lax.broadcasted_iota(jnp.int32, shape, dim)


def fetch(sources, targets, sems):
    copies = [
        pltpu.make_async_copy(source, target, sems.at[i])
        for i, (source, target) in enumerate(zip(sources, targets))
    ]
    for copy in copies:
        copy.start()
    for copy in copies:
        copy.wait()


def pack_kernel(own_hbm, queue_hbm, to_below, to_above, base, own, slots, queue, sems):
    fetch([own_hbm, queue_hbm], [own, queue], sems)
    x = pltpu.roll(own[...].astype(F32).reshape(48, 8, 128), 2, 1)
    row = iota((48, 8, 128), 1)
    put = (iota((16, 384), 0) == iota((16, 384), 1) % 128 - iota((16, 384), 1) // 128 * 16).astype(BF16)
    placed = jnp.dot(queue[...].reshape(48, 16), put, preferred_element_type=F32)
    slots[...] = jnp.zeros_like(slots)
    slots[pl.ds(4, 48, stride=8), :] = placed[:, :128]
    y = jnp.where(row < 2, x, slots[...].reshape(48, 8, 128))
    to_below[...] = y.astype(BF16).reshape(3, 16, 8, 128)
    slots[pl.ds(4, 48, stride=8), :] = jnp.zeros((48, 128), F32)
    slots[pl.ds(5, 48, stride=8), :] = placed[:, 256:]
    y = jnp.where((row >= 2) & (row < 4), x, slots[...].reshape(48, 8, 128))
    to_above[...] = y.astype(BF16).reshape(3, 16, 8, 128)
    base[...] = placed[:, 128:256]


def middle_kernel(
    blend_hbm, own, from_above, from_below, base, maps, rim, ask, back, both, blend, sems
):
    copy = pltpu.make_async_copy(blend_hbm, blend, sems.at[0])
    copy.start()
    x = from_above[...].astype(F32) + from_below[...].astype(F32)
    rim[...] = x.astype(BF16)
    both[...] = x.reshape(384, 128)
    three = both[pl.ds(4, 48, stride=8), :] + both[pl.ds(5, 48, stride=8), :] + base[...]
    three = three.astype(BF16)
    for i in range(ask.shape[0]):
        ask[i] = three
    copy.wait()
    row = iota((8, 128), 0)
    for ch in range(3):
        for f in range(8):
            y = x[ch, f]
            y = jnp.where(row == 6, blend[0, f].astype(F32), y)
            y = jnp.where(row == 7, blend[1, f].astype(F32), y)
            both_rows = jnp.concatenate([own[ch, f].astype(F32), y], axis=0)
            back[ch, f] = both_rows.astype(BF16)


def prepare_kernel(*refs):
    sources, (w_in, w_mid, w_mix, w_out, maps), targets = refs[:7], refs[7:12], refs[12:19]
    fetch(sources, targets, refs[19])
    taps, win, bias, wmid, mix, wout, over = targets
    col = iota((128, 384), 0)
    lane = iota((128, 384), 1)
    pixel = lane & 127
    maps[:, 0:384] = (col == (pixel & 15) * 8 + (pixel >> 4) + (lane >> 7) - 1).astype(BF16)
    maps[:, 384:768] = (col == (lane >> 7) * 16 + (pixel >> 3)).astype(BF16)
    col = iota((128, 128), 0)
    maps[:, 768:896] = (iota((128, 128), 1) == (col & 15) * 8 + (col >> 4)).astype(BF16)
    k = iota((256, 128), 0)
    low = (k % 80 >= 48) & (k % 80 < 72) & (k % 8 >= 3) & (k % 8 < 6) & (k < 240)
    b = bias[...]
    b0 = b.astype(BF16).astype(F32)
    b1 = (b - b0).astype(BF16).astype(F32)
    b2 = b - b0 - b1
    pad = jnp.zeros((2, 128), F32)
    w = [jnp.concatenate([win[i].astype(F32), pad], axis=0) for i in range(9)]
    w = jnp.concatenate(w, axis=0).astype(BF16)
    for q in range(5):
        for e in range(2):
            v = jnp.dot(taps[2 * q + e], w, preferred_element_type=F32)
            v = jnp.where(low, v - v.astype(BF16).astype(F32), v)
            v = jnp.where(k == 152, b0, jnp.where(k == 153, b1, jnp.where(k == 154, b2, v)))
            w_in[q, :, e * 128 : (e + 1) * 128] = v.astype(BF16)
    none = jnp.zeros((128, 384), BF16)
    w_mid[0:128, 1152:1536] = none
    w_mid[128:256, 0:384] = none
    for dr in range(3):
        for dv in range(3):
            t = wmid[dr * 3 + dv].T
            for e in range(2):
                tap = (dr + e) * 3 + dv
                w_mid[e * 128 : (e + 1) * 128, tap * 128 : (tap + 1) * 128] = t
    flat = mix[...].reshape(256, 128)
    flat = jnp.concatenate([flat[:128].T, flat[128:].T], axis=1)
    same = iota((128, 256), 0) % 16 == iota((128, 256), 1) % 16
    for p in range(16):
        t = jnp.dot(flat, over[240 - 16 * p : 496 - 16 * p, :], preferred_element_type=F32)
        t = jnp.where(same, t, 0.0).astype(BF16)
        for g in range(8):
            w_mix[g, p * 16 : (p + 1) * 16, :] = t[g * 16 : (g + 1) * 16, :]
    own = iota((16, 256), 0) == iota((16, 256), 1) // 16
    wo = jnp.concatenate([wout[...].astype(F32), jnp.zeros((5, 128), F32)], axis=0).astype(BF16)
    for g in range(8):
        pick = (iota((128, 256), 0) == g * 16 + iota((128, 256), 1) % 16).astype(BF16)
        t = jnp.dot(wo, pick, preferred_element_type=F32)
        for o in range(3):
            w_out[g, o * 16 : (o + 1) * 16, :] = jnp.where(own, t[o : o + 1, :], 0.0).astype(BF16)


def lift(frame_slot, queue, maps, first, count):
    j = iota((8, 384), 0)
    lane = iota((8, 384), 1) - j % 3 * 16
    start = lax.axis_index("tm") * 16 + first
    hot = []
    for f in range(count):
        slot = frame_slot[jnp.minimum(start + f, 127)]
        place = slot // 16 * 48 + slot % 16
        hot.append(jnp.where((lane == place) & (j < 6), 1.0, 0.0))
    hot = jnp.concatenate(hot, axis=0).astype(BF16)
    chosen = jnp.dot(hot, queue[...].reshape(384, 128), preferred_element_type=F32).astype(BF16)
    return jnp.dot(chosen, maps[:, 384:768], preferred_element_type=F32)


def tiles_of(own, rim, lifted):
    tiles = own + rim + [lifted[:, br * 128 : (br + 1) * 128] for br in range(3)]
    return jnp.concatenate(tiles + [jnp.ones((8, 128), F32)], axis=0).astype(BF16)


def stage(inputs, at, frames, maps):
    x = jnp.concatenate(frames, axis=0)
    x = jnp.dot(x, maps[:, 0:384], preferred_element_type=F32).astype(BF16)
    for f in range(len(frames)):
        for dv in range(3):
            inputs[at + f, dv * 80 : (dv + 1) * 80, :] = x[
                f * 80 : (f + 1) * 80, dv * 128 : (dv + 1) * 128
            ]
        inputs[at + f, 240:256, :] = jnp.zeros((16, 128), BF16)


def gains(gain):
    r = lax.axis_index("rows")
    top = jnp.where(r > 0, 0.5, 0.0)
    bottom = jnp.where(r < lax.axis_size("rows") - 1, 0.5, 0.0)
    g = gain[...]
    out = []
    for q in range(5):
        first = g * (top if q == 0 else 0.5)
        second = g * (bottom if q == 4 else 0.5)
        out.append(jnp.concatenate([first, second], axis=1))
    return out


def spread_inputs(inputs, pair):
    return jnp.concatenate([inputs[pair * 2 + b].T for b in range(2)], axis=0)


def norm_act(h, gain, act, q):
    sq = h * h
    parts = []
    for e in range(2):
        lanes = slice(e * 128, (e + 1) * 128)
        ss = jnp.sum(sq[:, lanes], axis=1, keepdims=True)
        scale = lax.rsqrt(ss * (1 / 128) + 1e-6)
        u = h[:, lanes] * scale * gain[:, lanes]
        parts.append(u * jnp.tanh(u) + u)
    s = iota((16, 128), 0)
    for e in range(2):
        a = parts[e].reshape(2, 128, 128)
        act[:, 2 * q + e, 1:9] = a.astype(BF16).reshape(2, 8, 16, 128)
        for b in range(2):
            left = jnp.where(s == 0, 0.0, pltpu.roll(a[b, 112:128], 1, 0))
            right = jnp.where(s == 15, 0.0, pltpu.roll(a[b, 0:16], 15, 0))
            act[b, 2 * q + e, 0] = left.astype(BF16)
            act[b, 2 * q + e, 9] = right.astype(BF16)


def mid_conv(act, w_mid, spatial, at, i):
    frames = []
    for b in range(2):
        taps = [
            act[b, 2 * i + dr, dv : dv + 8].reshape(128, 128) for dr in range(4) for dv in range(3)
        ]
        frames.append(jnp.concatenate(taps, axis=1))
    x = jnp.concatenate(frames, axis=0)
    y = lax.dot_general(w_mid[...], x, NT, preferred_element_type=F32).astype(BF16)
    for b in range(2):
        for e in range(2):
            spatial[i, at + b, :, e * 128 : (e + 1) * 128] = y[
                e * 128 : (e + 1) * 128, b * 128 : (b + 1) * 128
            ]


def network(inputs, pairs, w_in, w_mid, gain, act0, act1, spatial):
    def step(done, pair, todo, following):
        if todo is not None:
            depth = spread_inputs(inputs, following)
            h = jnp.dot(depth, w_in[0], preferred_element_type=F32)
        for q in range(5):
            if done is not None and q < 4:
                mid_conv(done, w_mid, spatial, pair * 2, q)
            if todo is not None:
                now = h
                if q < 4:
                    h = jnp.dot(depth, w_in[q + 1], preferred_element_type=F32)
                norm_act(now, gain[q], todo, q)

    step(None, None, act0, 0)

    @pl.loop(0, pairs // 2 - 1)
    def _(k):
        step(act0, 2 * k, act1, 2 * k + 1)
        step(act1, 2 * k + 1, act0, 2 * k + 2)

    step(act0, pairs - 2, act1, pairs - 1)
    step(act1, pairs - 1, None, None)


def predict(halves, w_mix, w_out, bias_out, total):
    @pl.loop(0, 4)
    def _(i):
        def mixed(g):
            rows = slice(g * 16, (g + 1) * 16)
            x = [ref[i, at : at + 8, rows, :].reshape(128, 256) for ref, at in halves]
            x = jnp.concatenate(x, axis=0)
            return jnp.dot(w_mix[g], x, preferred_element_type=F32) + x.astype(F32)

        acc = None
        following = mixed(0)
        for g in range(8):
            now = following
            if g < 7:
                following = mixed(g + 1)
            h = 0.5 * now
            outer = (h * jnp.tanh(h) + h).astype(BF16)
            p = jnp.dot(w_out[g], outer, preferred_element_type=F32)
            acc = p if acc is None else acc + p
        for o in range(3):
            part = acc[o * 16 : (o + 1) * 16, :] + bias_out[o]
            for e in range(2):
                total[2 * i + e, o * 16 : (o + 1) * 16, :] = part[:, e * 128 : (e + 1) * 128]


def unorder(total, maps, rows):
    x = total[...].reshape(384, 128)
    x0 = x.astype(BF16)
    r = x - x0.astype(F32)
    x1 = r.astype(BF16)
    x2 = (r - x1.astype(F32)).astype(BF16)
    y = [jnp.dot(part, maps[:, 768:896], preferred_element_type=F32) for part in (x0, x1, x2)]
    rows[...] = y[0] + (y[1] + y[2])


def picture(rows, o, f):
    return rows[pl.ds(o * 16 + f, 8, stride=48), :]


def own_kernel(
    frame_slot, own, rim, queue, gain, w_in, w_mid, maps, spatial, inputs, act0, act1
):
    lifted = lift(frame_slot, queue, maps, 0, 16)
    for part in range(4):
        frames = []
        for f in range(part * 4, part * 4 + 4):
            noisy = [own[ch, f].astype(F32) for ch in range(3)]
            edge = [rim[ch, f].astype(F32) for ch in range(3)]
            frames.append(tiles_of(noisy, edge, lifted[f * 8 : f * 8 + 8]))
        stage(inputs, part * 4, frames, maps)
    network(inputs, 8, w_in, w_mid, gains(gain), act0, act1, spatial)


def late_kernel(
    frame_slot, bias_out, ahead, queue, gain, w_in, w_mid, maps, w_mix, w_out, own,
    send, near, inputs, act0, act1, spatial, total, rows,
):
    lifted = lift(frame_slot, queue, maps, 16, 8)
    for part in range(2):
        frames = []
        for f in range(part * 4, part * 4 + 4):
            x = [ahead[ch, f].astype(F32) for ch in range(3)]
            frames.append(
                tiles_of([tile[:8] for tile in x], [tile[8:] for tile in x], lifted[f * 8 : f * 8 + 8])
            )
        stage(inputs, part * 4, frames, maps)
    network(inputs, 4, w_in, w_mid, gains(gain), act0, act1, spatial)
    predict([(own, 8), (spatial, 0)], w_mix, w_out, bias_out, total)
    unorder(total, maps, rows)
    for f in range(8):
        w = ahead[0, f].astype(F32)
        share = w[15:16] / jnp.maximum(w[14:15] + w[15:16], 1.0)
        for o in range(3):
            near[o, f] = picture(rows, o, f)
            send[o, f] = (picture(rows, o, f + 8) * share).astype(BF16)


def early_kernel(bias_out, blend, maps, w_mix, w_out, own, near, mine, total, rows):
    predict([(own, 0), (own, 8)], w_mix, w_out, bias_out, total)
    unorder(total, maps, rows)
    t = lax.axis_index("tm")
    has_prev = jnp.where(t > 0, 1.0, 0.0)
    has_next = jnp.where(t < lax.axis_size("tm") - 1, 1.0, 0.0)
    one = jnp.ones((8, 128), F32)
    for f in range(8):
        lead = one * blend[0, f].astype(F32)
        share = lead / (lead + one * (blend[1, f].astype(F32) * has_prev))
        lead = one * (blend[0, f + 8].astype(F32) * has_next)
        trail = one * blend[1, f + 8].astype(F32)
        for o in range(3):
            mine[o, f] = picture(rows, o, f) * share
            mine[o, f + 8] = (lead * near[o, f] + trail * picture(rows, o, f + 8)) / (lead + trail)


def join_kernel(mine, arrived, out):
    out[:, 0:8] = mine[:, 0:8] + arrived[...].astype(F32)
    out[:, 8:16] = mine[:, 8:16]


def network_scratch(frames):
    act = pltpu.VMEM((2, 10, 10, 16, 128), BF16)
    return [pltpu.VMEM((frames, 256, 128), BF16), act, act]


PICTURES = [pltpu.VMEM((8, 48, 128), F32), pltpu.VMEM((384, 128), F32)]


def shape(dims, kind):
    return jax.ShapeDtypeStruct(dims, kind)


def call(kernel, name, scalars, arrays, outs, scratch_shapes=(), flops=10**8, space=VMEM):
    if space is HBM:
        arrays = [pltpu.with_memory_space_constraint(a, pltpu.HBM) for a in arrays]
    return pl.pallas_call(
        kernel,
        out_shape=outs,
        in_specs=[SMEM] * len(scalars) + [space] * len(arrays),
        out_specs=tuple(VMEM for _ in outs),
        scratch_shapes=list(scratch_shapes),
        compiler_params=PARAMS,
        cost_estimate=pl.CostEstimate(flops=flops, bytes_accessed=10**6, transcendentals=0),
        name=name,
    )(*scalars, *arrays)


def copies_of(arrays):
    return [pltpu.VMEM(a.shape, a.dtype) for a in arrays] + [pltpu.SemaphoreType.DMA((len(arrays),))]


def body(
    noisy_frames, base_queue, frame_slot, blend_weight, weight_in, bias_in, gain_mid, weight_mid,
    time_mix, weight_out, bias_out,
):
    n_t = lax.axis_size("tm")
    n_r = lax.axis_size("rows")
    down = [(i, i + 1) for i in range(n_r - 1)]
    up = [(i + 1, i) for i in range(n_r - 1)]
    back = [(i + 1, i) for i in range(n_t - 1)]
    forth = [(i, i + 1) for i in range(n_t - 1)]
    blend = blend_weight.T
    tile = shape((3, 16, 8, 128), BF16)

    raw = [noisy_frames, jnp.transpose(base_queue[:, :, 0, :], (1, 0, 2))]
    to_below, to_above, base, own = call(
        pack_kernel,
        "pack",
        [],
        raw,
        (tile, tile, shape((48, 128), F32), tile),
        [pltpu.VMEM((384, 128), F32)] + copies_of(raw)[1:],
        space=HBM,
    )
    from_above = lax.ppermute(to_below, "rows", down)
    from_below = lax.ppermute(to_above, "rows", up)
    raw = [
        jnp.asarray(tap_matrix(), BF16),
        weight_in.reshape(9, 6, 128),
        bias_in.reshape(1, 128),
        weight_mid.reshape(9, 128, 128),
        jnp.transpose(time_mix, (1, 2, 0)),
        weight_out.T,
        jnp.asarray(spread_matrix(), BF16),
    ]
    w_in, w_mid, w_mix, w_out, maps = call(
        prepare_kernel,
        "prepare",
        [],
        raw,
        (
            shape((5, 256, 256), BF16),
            shape((256, 1536), BF16),
            shape((8, 256, 256), BF16),
            shape((8, 48, 256), BF16),
            shape((128, 896), BF16),
        ),
        copies_of(raw),
        flops=2 * 10**9,
        space=HBM,
    )
    rim, ask, pack = pl.pallas_call(
        middle_kernel,
        out_shape=(tile, shape((n_t, 48, 128), BF16), shape((3, 8, 16, 128), BF16)),
        in_specs=[HBM] + [VMEM] * 5,
        out_specs=(VMEM,) * 3,
        scratch_shapes=[
            pltpu.VMEM((384, 128), F32),
            pltpu.SMEM((2, 16), jnp.int32),
            pltpu.SemaphoreType.DMA((1,)),
        ],
        compiler_params=PARAMS,
        name="middle",
    )(pltpu.with_memory_space_constraint(blend, pltpu.HBM), own, from_above, from_below, base, maps)
    queue = lax.all_to_all(ask, "tm", 0, 0, tiled=True)
    ahead = lax.ppermute(pack, "tm", back)
    gain = gain_mid.reshape(1, 128)
    (spatial,) = call(
        own_kernel,
        "own",
        [frame_slot],
        [own, rim, queue, gain, w_in, w_mid, maps],
        (shape((4, 16, 128, 256), BF16),),
        network_scratch(16),
        flops=10**10,
    )
    send, near = call(
        late_kernel,
        "late",
        [frame_slot, bias_out],
        [ahead, queue, gain, w_in, w_mid, maps, w_mix, w_out, spatial],
        (shape((3, 8, 8, 128), BF16), shape((3, 8, 8, 128), F32)),
        network_scratch(8) + [pltpu.VMEM((4, 8, 128, 256), BF16)] + PICTURES,
        flops=10**10,
    )
    arrived = lax.ppermute(send, "tm", forth)
    (mine,) = call(
        early_kernel,
        "early",
        [bias_out, blend],
        [maps, w_mix, w_out, spatial, near],
        (shape((3, 16, 8, 128), F32),),
        PICTURES,
        flops=5 * 10**9,
    )
    (out,) = call(join_kernel, "join", [], [mine, arrived], (shape((3, 16, 8, 128), F32),))
    return out


def solution(mesh):
    return jax.shard_map(
        body,
        mesh=mesh,
        in_specs=(
            P(None, "tm", "rows", None),
            P("tm", None, "rows", None),
            P(),
            P("tm", None),
            P(),
            P(),
            P(),
            P(),
            P(),
            P(),
            P(),
        ),
        out_specs=P(None, "tm", "rows", None),
        check_vma=False,
    )
```

time: 211 us -> 57.5 us (0.27); the launches traced: 207 us -> 57.2 us
  matrix products: 70.1 us -> 0 us
  local copies, waits for them, and re-layouts: 48 us -> 0.02 us
  Pallas kernels: 0 us -> 30 us
  waiting for transfers between devices: 33.6 us -> 8.15 us
  blocking collectives: 22.3 us -> 0 us
  other arithmetic: 8.77 us -> 0 us
  starting transfers between devices: 24 us -> 18.9 us
    dot_general x4 -> x0, matrix products: 42.2 us -> none  [the longest x2 28.9 us: predict(): jnp.einsum('co,cfrw->ofrw', weight_out, outer, preferred_element_type=jnp...]
    pallas_call x0 -> x7, Pallas kernels: none -> 30 us  [the longest x6 28.7 us: call(): pl.pallas_call(kernel, out_shape=outs, in_specs=[SMEM] * len(scalars) + [...]
    conv_general_dilated x2 -> x0, matrix products: 27.9 us -> none  [conv_rows(): lax.conv_general_dilated(source, weight, (1, 1), ((0, 0), (1, 1)), dimens...]
    ppermute x6 -> x4, waiting for transfers between devices: 33.6 us -> 7.12 us  [the longest x1 7.12 us: body(): from_below = lax.ppermute(to_above, 'rows', up)]
    all_gather x1 -> x0, blocking collectives: 22.3 us -> none  [body(): queue_all = lax.all_gather(base_queue, 'tm', axis=0, tiled=True)]
    slice x9 -> x0, local copies, waits for them, and re-layouts: 20.6 us -> none  [the longest x2 11.8 us: body(): second_pred = predict(spatial[:, half:], time_mix, weight_out, bias_out)]
    dot_general x4 -> x0, local copies, waits for them, and re-layouts: 19.6 us -> none  [the longest x2 18.6 us: predict(): jnp.einsum('cfg,cgrw->cfrw', time_mix, spatial, preferred_element_type=jn...]
    ppermute x6 -> x4, starting transfers between devices: 24 us -> 14.6 us  [the longest x1 6.33 us: body(): from_above = lax.ppermute(to_below, 'rows', down)]
  transfers between devices with their start and end apart: 6 -> 5, of which waited for: 5 -> 2; matrix products, arithmetic and copies ran while one was open for 2% -> 0% of each run, Pallas kernels for 0% -> 30%
where the time goes in v2:
time: 57.5 us; the launch traced here: 57.2 us
  Pallas kernels  30 us (52%)
  starting transfers between devices  18.9 us (33%)
  waiting for transfers between devices  8.15 us (14%)
    pallas_call x6, Pallas kernels, call(): pl.pallas_call(kernel, out_shape=outs, in_specs=[SMEM] * len(scalars) + [...  28.7 us
    ppermute x1, waiting for transfers between devices, body(): from_below = lax.ppermute(to_above, 'rows', up)  7.12 us
    ppermute x1, starting transfers between devices, body(): from_above = lax.ppermute(to_below, 'rows', down)  6.33 us
    all_to_all x1, starting transfers between devices, body(): queue = lax.all_to_all(ask, 'tm', 0, 0, tiled=True)  4.23 us
    ppermute x1, starting transfers between devices, body(): arrived = lax.ppermute(send, 'tm', forth)  3.92 us
    ppermute x1, starting transfers between devices, body(): ahead = lax.ppermute(pack, 'tm', back)  2.47 us
    ppermute x1, starting transfers between devices, body(): from_below = lax.ppermute(to_above, 'rows', up)  1.92 us
    pallas_call x1, Pallas kernels, body(): pl.pallas_call(middle_kernel, out_shape=(tile, shape((n_t, 48, 128), BF16...  1.34 us
  transfers between devices with their start and end apart: 5, of which 2 were waited for; matrix products, arithmetic and copies ran while one was open for 0% of the time, Pallas kernels for 30%

profile of v2, /device:TPU:95, one launch (start us, length us, event | category | flops | bytes accessed | tf_op | source)
XLA Modules:
  0.0 57.2 jit_solution(8727539411969921575)
XLA Ops:
  0.0 0.0 copy-start.1
  0.0 0.0 copy-start.2
  0.0 1.1 %pack.1 = (bf16[3,16,8,128]{3,2,1,0:T(8,128)(2,1)S(1)}, bf16[3,16,8,128]{3,2,1,0:T(8,128)(2,1)S(1)}, f32[48,128]{1,0:T(8,128)S(1)}, bf16[3,16,8,128]{3,2,1,0:T(8,128)(2,1)S(1)}) custom-call(bf16[3,16,8,128]{3,2,1,0:T(8,128)(2,1)} %own_hbm.1, bf16[3,16,16]{2,1,0:T(8,128)(2,1)} %bitcast.17), custom_call_target="tpu_custom_call" | custom-call | flops 100000000 | bytes 1000000 | tf_op jit(solution)/shard_map/pack/pallas_call | solution.py:377
  1.1 6.3 %collective-permute-start = (bf16[3,16,8,128]{3,2,1,0:T(8,128)(2,1)S(1)}, bf16[3,16,8,128]{3,2,1,0:T(8,128)(2,1)S(1)}, u32[]{:S(2)}, u32[]{:S(2)}) collective-permute-start(bf16[3,16,8,128]{3,2,1,0:T(8,128)(2,1)S(1)} %get-tuple-element.23), channel_id=1, source_target_pairs={{0,1},{1,2},{2,3},{3,4},{4,5},{5,6},{6,7},{7,8},{8,9},{9,10},{10,1... | collective-permute-start | bytes 294920 | tf_op jit(solution)/shard_map/ppermute | solution.py:416
  7.5 1.9 %collective-permute-start.1 = (bf16[3,16,8,128]{3,2,1,0:T(8,128)(2,1)S(1)}, bf16[3,16,8,128]{3,2,1,0:T(8,128)(2,1)S(1)}, u32[]{:S(2)}, u32[]{:S(2)}) collective-permute-start(bf16[3,16,8,128]{3,2,1,0:T(8,128)(2,1)S(1)} %get-tuple-element.24), channel_id=1, source_target_pairs={{1,0},{2,1},{3,2},{4,3},{5,4},{6,5},{7,6},{8,7},{9,8},{10,9},{11,1... | collective-permute-start | bytes 294920 | tf_op jit(solution)/shard_map/ppermute | solution.py:417
  9.4 2.1 %prepare.1 = (bf16[5,256,256]{2,1,0:T(8,128)(2,1)S(1)}, bf16[256,1536]{1,0:T(8,128)(2,1)S(1)}, bf16[8,256,256]{2,1,0:T(8,128)(2,1)S(1)}, bf16[8,48,256]{2,1,0:T(8,128)(2,1)S(1)}, bf16[128,896]{1,0:T(8,128)(2,1)S(1)}) custom-call(bf16[10,256,72]{2,1,0:T(8,128)(2,1)} %constant.4.clone.refs_0_, bf16[9,6,128]{2,1,0:T(8,128)(2,1)} %bitcast.16, ...), custom_call_target="tpu_custom_call" | custom-call | flops 2000000000 | bytes 1000000 | tf_op jit(solution)/shard_map/prepare/pallas_call | solution.py:377
  11.5 0.0 collective-permute-done.from_above
  11.5 7.1 %collective-permute-done.1.from_below = bf16[3,16,8,128]{3,2,1,0:T(8,128)(2,1)S(1)} collective-permute-done((bf16[3,16,8,128]{3,2,1,0:T(8,128)(2,1)S(1)}, bf16[3,16,8,128]{3,2,1,0:T(8,128)(2,1)S(1)}, u32[]{:S(2)}, u32[]{:S(2)}) %collective-permute-start.1) | collective-permute-done | bytes 98336 | tf_op jit(solution)/shard_map/ppermute | solution.py:417
  18.7 1.3 %middle.1 = (bf16[3,16,8,128]{3,2,1,0:T(8,128)(2,1)S(1)}, bf16[8,48,128]{2,1,0:T(8,128)(2,1)}, bf16[3,8,16,128]{3,2,1,0:T(8,128)(2,1)S(1)}) custom-call(s32[2,16]{1,0:T(2,128)} %bitcast.10, bf16[3,16,8,128]{3,2,1,0:T(8,128)(2,1)S(1)} %get-tuple-element.22.own, bf16[3,16,8,128]{3,2,1,0:T(8,128)(2,1)S(1)} %collective-permute-done.from_above, ...), custom_call_target="tpu_custom_call" | custom-call | tf_op jit(solution)/shard_map/middle/pallas_call | solution.py:443
  20.0 4.2 %all-to-all-start = ((bf16[8,48,128]{2,1,0:T(8,128)(2,1)}), bf16[8,48,128]{2,1,0:T(8,128)(2,1)S(1)}, u32[]{:S(2)}, u32[]{:S(2)}) async-start(bf16[8,48,128]{2,1,0:T(8,128)(2,1)} %get-tuple-element.27), calls=%async_computation | async-start | bytes 196608 | tf_op jit(solution)/shard_map/all_to_all | solution.py:456
  24.2 2.5 %collective-permute-start.2 = (bf16[3,8,16,128]{3,2,1,0:T(8,128)(2,1)S(1)}, bf16[3,8,16,128]{3,2,1,0:T(8,128)(2,1)S(1)}, u32[]{:S(2)}, u32[]{:S(2)}) collective-permute-start(bf16[3,8,16,128]{3,2,1,0:T(8,128)(2,1)S(1)} %get-tuple-element.30), channel_id=1, source_target_pairs={{32,0},{64,32},{96,64},{128,96},{160,128},{192,160},{224,192},{33,... | collective-permute-start | bytes 294920 | tf_op jit(solution)/shard_map/ppermute | solution.py:457
  26.7 1.0 %all-to-all-done.queue = bf16[8,48,128]{2,1,0:T(8,128)(2,1)S(1)} async-done(((bf16[8,48,128]{2,1,0:T(8,128)(2,1)}), bf16[8,48,128]{2,1,0:T(8,128)(2,1)S(1)}, u32[]{:S(2)}, u32[]{:S(2)}) %all-to-all-start) | async-done | bytes 98336 | tf_op jit(solution)/shard_map/all_to_all | solution.py:456
  27.7 0.0 copy-done.1
  27.7 0.0 copy-done.2
  27.8 0.0 copy-start.3
  27.8 10.7 %own.1 = bf16[4,16,128,256]{3,2,1,0:T(8,128)(2,1)S(1)} custom-call(s32[128]{0:T(128)S(1)} %copy-done.1, bf16[3,16,8,128]{3,2,1,0:T(8,128)(2,1)S(1)} %get-tuple-element.22.own, bf16[3,16,8,128]{3,2,1,0:T(8,128)(2,1)S(1)} %get-tuple-element.26.rim, bf16[8,48,128]{2,1,0:T(8,128)(2,1)S(1)} %all-to-all-done.queue, f32[1,128]{1,0:T(1,128)S(1)} %bitcast.12, ...), custom_call_target="tpu_custom_call" | custom-call | flops 10000000000 | bytes 1000000 | tf_op jit(solution)/shard_map/own/pallas_call | solution.py:377
  38.5 0.0 collective-permute-done.2.ahead
  38.5 0.0 copy-done.3
  38.5 0.0 copy-start
  38.5 9.4 %late.1 = (bf16[3,8,8,128]{3,2,1,0:T(8,128)(2,1)S(1)}, f32[3,8,8,128]{3,2,1,0:T(8,128)S(1)}) custom-call(s32[128]{0:T(128)S(1)} %copy-done.1, f32[3]{0:T(128)S(1)} %copy-done.3, bf16[3,8,16,128]{3,2,1,0:T(8,128)(2,1)S(1)} %collective-permute-done.2.ahead, bf16[8,48,128]{2,1,0:T(8,128)(2,1)S(1)} %all-to-all-done.queue, f32[1,128]{1,0:T(1,128)S(1)} %bitcast.13, ...), custom_call_target="tpu_custom_call" | custom-call | flops 10000000000 | bytes 1000000 | tf_op jit(solution)/shard_map/late/pallas_call | solution.py:377
  47.9 3.9 %collective-permute-start.3 = (bf16[3,8,8,128]{3,2,1,0:T(8,128)(2,1)S(1)}, bf16[3,8,8,128]{3,2,1,0:T(8,128)(2,1)S(1)}, u32[]{:S(2)}, u32[]{:S(2)}) collective-permute-start(bf16[3,8,8,128]{3,2,1,0:T(8,128)(2,1)S(1)} %get-tuple-element.32), channel_id=1, source_target_pairs={{0,32},{32,64},{64,96},{96,128},{128,160},{160,192},{192,224},{1,3... | collective-permute-start | bytes 147464 | tf_op jit(solution)/shard_map/ppermute | solution.py:477
  51.9 0.0 copy-done
  51.9 4.6 %early.1.mine = f32[3,16,8,128]{3,2,1,0:T(8,128)S(1)} custom-call(f32[3]{0:T(128)S(1)} %copy-done.3, s32[2,16]{1,0:T(2,128)S(1)} %bitcast.11, bf16[128,896]{1,0:T(8,128)(2,1)S(1)} %get-tuple-element.19.maps, bf16[8,256,256]{2,1,0:T(8,128)(2,1)S(1)} %get-tuple-element.20.w_mix, bf16[8,48,256]{2,1,0:T(8,128)(2,1)S(1)} %get-tuple-element.21.w_out, ...), custom_call_target="tpu_custom_call" | custom-call | flops 5000000000 | bytes 1000000 | tf_op jit(solution)/shard_map/early/pallas_call | solution.py:377
  56.5 0.0 collective-permute-done.3.arrived
  56.5 0.7 %join.1 = f32[3,16,8,128]{3,2,1,0:T(8,128)} custom-call(f32[3,16,8,128]{3,2,1,0:T(8,128)S(1)} %early.1.mine, bf16[3,8,8,128]{3,2,1,0:T(8,128)(2,1)S(1)} %collective-permute-done.3.arrived), custom_call_target="tpu_custom_call" | custom-call | flops 100000000 | bytes 1000000 | tf_op jit(solution)/shard_map/join/pallas_call | solution.py:377
Async XLA Ops:
  0.0 27.7 %copy-start.1 = (s32[128]{0:T(128)S(1)}, s32[128]{0:T(128)}, u32[]{:S(2)}) copy-start(s32[128]{0:T(128)} %frame_slot.3) | copy-start | bytes 1540
  0.0 27.7 %copy-start.2 = (f32[128]{0:T(128)S(1)}, f32[128]{0:T(128)}, u32[]{:S(2)}) copy-start(f32[128]{0:T(128)} %param.19) | copy-start | bytes 1540
  1.1 10.4 %collective-permute-start = (bf16[3,16,8,128]{3,2,1,0:T(8,128)(2,1)S(1)}, bf16[3,16,8,128]{3,2,1,0:T(8,128)(2,1)S(1)}, u32[]{:S(2)}, u32[]{:S(2)}) collective-permute-start(bf16[3,16,8,128]{3,2,1,0:T(8,128)(2,1)S(1)} %get-tuple-element.23), channel_id=1, source_target_pairs={{0,1},{1,2},{2,3},{3,4},{4,5},{5,6},{6,7},{7,8},{8,9},{9,10},{10,1... | collective-permute-start | bytes 294920 | tf_op jit(solution)/shard_map/ppermute | solution.py:416
  7.5 11.2 %collective-permute-start.1 = (bf16[3,16,8,128]{3,2,1,0:T(8,128)(2,1)S(1)}, bf16[3,16,8,128]{3,2,1,0:T(8,128)(2,1)S(1)}, u32[]{:S(2)}, u32[]{:S(2)}) collective-permute-start(bf16[3,16,8,128]{3,2,1,0:T(8,128)(2,1)S(1)} %get-tuple-element.24), channel_id=1, source_target_pairs={{1,0},{2,1},{3,2},{4,3},{5,4},{6,5},{7,6},{8,7},{9,8},{10,9},{11,1... | collective-permute-start | bytes 294920 | tf_op jit(solution)/shard_map/ppermute | solution.py:417
  20.0 7.7 %all-to-all-start = ((bf16[8,48,128]{2,1,0:T(8,128)(2,1)}), bf16[8,48,128]{2,1,0:T(8,128)(2,1)S(1)}, u32[]{:S(2)}, u32[]{:S(2)}) async-start(bf16[8,48,128]{2,1,0:T(8,128)(2,1)} %get-tuple-element.27), calls=%async_computation | async-start | bytes 196608 | tf_op jit(solution)/shard_map/all_to_all | solution.py:456
  24.2 14.2 %collective-permute-start.2 = (bf16[3,8,16,128]{3,2,1,0:T(8,128)(2,1)S(1)}, bf16[3,8,16,128]{3,2,1,0:T(8,128)(2,1)S(1)}, u32[]{:S(2)}, u32[]{:S(2)}) collective-permute-start(bf16[3,8,16,128]{3,2,1,0:T(8,128)(2,1)S(1)} %get-tuple-element.30), channel_id=1, source_target_pairs={{32,0},{64,32},{96,64},{128,96},{160,128},{192,160},{224,192},{33,... | collective-permute-start | bytes 294920 | tf_op jit(solution)/shard_map/ppermute | solution.py:457
  27.8 10.7 %copy-start.3 = (f32[3]{0:T(128)S(1)}, f32[3]{0:T(128)}, u32[]{:S(2)}) copy-start(f32[3]{0:T(128)} %bias_out.3) | copy-start | bytes 40
  38.5 13.4 %copy-start = (s32[16,2]{0,1:T(2,128)S(1)}, s32[16,2]{0,1:T(2,128)}, u32[]{:S(2)}) copy-start(s32[16,2]{0,1:T(2,128)} %param.16) | copy-start | bytes 388
  47.9 8.5 %collective-permute-start.3 = (bf16[3,8,8,128]{3,2,1,0:T(8,128)(2,1)S(1)}, bf16[3,8,8,128]{3,2,1,0:T(8,128)(2,1)S(1)}, u32[]{:S(2)}, u32[]{:S(2)}) collective-permute-start(bf16[3,8,8,128]{3,2,1,0:T(8,128)(2,1)S(1)} %get-tuple-element.32), channel_id=1, source_target_pairs={{0,32},{32,64},{64,96},{96,128},{128,160},{160,192},{192,224},{1,3... | collective-permute-start | bytes 147464 | tf_op jit(solution)/shard_map/ppermute | solution.py:477

commit v3 on v2

--- a/solution.py
+++ b/solution.py
@@ -60,33 +60,40 @@
         copy.wait()
 
 
-def pack_kernel(own_hbm, queue_hbm, to_below, to_above, base, own, slots, queue, sems):
+def pack_kernel(own_hbm, queue_hbm, to_near, to_far, base, own, wide, queue, sems):
     fetch([own_hbm, queue_hbm], [own, queue], sems)
-    x = pltpu.roll(own[...].astype(F32).reshape(48, 8, 128), 2, 1)
-    row = iota((48, 8, 128), 1)
+    wide[...] = own[...].astype(F32).reshape(384, 128)
     put = (iota((16, 384), 0) == iota((16, 384), 1) % 128 - iota((16, 384), 1) // 128 * 16).astype(BF16)
     placed = jnp.dot(queue[...].reshape(48, 16), put, preferred_element_type=F32)
-    slots[...] = jnp.zeros_like(slots)
-    slots[pl.ds(4, 48, stride=8), :] = placed[:, :128]
-    y = jnp.where(row < 2, x, slots[...].reshape(48, 8, 128))
-    to_below[...] = y.astype(BF16).reshape(3, 16, 8, 128)
-    slots[pl.ds(4, 48, stride=8), :] = jnp.zeros((48, 128), F32)
-    slots[pl.ds(5, 48, stride=8), :] = placed[:, 256:]
-    y = jnp.where((row >= 2) & (row < 4), x, slots[...].reshape(48, 8, 128))
-    to_above[...] = y.astype(BF16).reshape(3, 16, 8, 128)
-    base[...] = placed[:, 128:256]
+    even = lax.rem(lax.axis_index("rows"), 2) == 0
+    parts = [
+        (wide[pl.ds(6, 48, stride=8), :], wide[pl.ds(0, 48, stride=8), :]),
+        (wide[pl.ds(7, 48, stride=8), :], wide[pl.ds(1, 48, stride=8), :]),
+        (placed[:, 0:128], placed[:, 256:384]),
+    ]
+    for k, (down, up) in enumerate(parts):
+        to_near[k * 48 : (k + 1) * 48, :] = jnp.where(even, down, up).astype(BF16)
+        to_far[k * 48 : (k + 1) * 48, :] = jnp.where(even, up, down).astype(BF16)
+    base[...] = placed[:, 128:256].astype(BF16)
 
 
 def middle_kernel(
-    blend_hbm, own, from_above, from_below, base, maps, rim, ask, back, both, blend, sems
+    blend_hbm, own, near, far, base, maps, rim, ask, back, both, blend, sems
 ):
     copy = pltpu.make_async_copy(blend_hbm, blend, sems.at[0])
     copy.start()
-    x = from_above[...].astype(F32) + from_below[...].astype(F32)
+    both[...] = jnp.zeros_like(both)
+    even = lax.rem(lax.axis_index("rows"), 2) == 0
+    for k in range(2):
+        x = near[k * 48 : (k + 1) * 48, :].astype(F32)
+        y = far[k * 48 : (k + 1) * 48, :].astype(F32)
+        both[pl.ds(k, 48, stride=8), :] = jnp.where(even, y, x)
+        both[pl.ds(k + 2, 48, stride=8), :] = jnp.where(even, x, y)
+    x = both[...].reshape(3, 16, 8, 128)
     rim[...] = x.astype(BF16)
-    both[...] = x.reshape(384, 128)
-    three = both[pl.ds(4, 48, stride=8), :] + both[pl.ds(5, 48, stride=8), :] + base[...]
-    three = three.astype(BF16)
+    three = near[96:144, :].astype(F32) + far[96:144, :].astype(F32)
+    three = three + base[...].astype(F32)
+    three = (three[:24] + pltpu.roll(three[24:], 64, 1)).astype(BF16)
     for i in range(ask.shape[0]):
         ask[i] = three
     copy.wait()
@@ -154,15 +161,18 @@
 
 def lift(frame_slot, queue, maps, first, count):
     j = iota((8, 384), 0)
-    lane = iota((8, 384), 1) - j % 3 * 16
+    lane = iota((8, 384), 1)
     start = lax.axis_index("tm") * 16 + first
     hot = []
     for f in range(count):
         slot = frame_slot[jnp.minimum(start + f, 127)]
-        place = slot // 16 * 48 + slot % 16
+        row = j % 3 * 16 + slot % 16
+        place = slot // 16 * 24 + jnp.where(row < 24, row, row + 168)
         hot.append(jnp.where((lane == place) & (j < 6), 1.0, 0.0))
     hot = jnp.concatenate(hot, axis=0).astype(BF16)
-    chosen = jnp.dot(hot, queue[...].reshape(384, 128), preferred_element_type=F32).astype(BF16)
+    rows = queue[...].astype(F32).reshape(192, 128)
+    rows = jnp.concatenate([rows, pltpu.roll(rows, 64, 1)], axis=0).astype(BF16)
+    chosen = jnp.dot(hot, rows, preferred_element_type=F32).astype(BF16)
     return jnp.dot(chosen, maps[:, 384:768], preferred_element_type=F32)
 
 
@@ -249,40 +259,40 @@
                     h = jnp.dot(depth, w_in[q + 1], preferred_element_type=F32)
                 norm_act(now, gain[q], todo, q)
 
+    acts = [act0, act1]
     step(None, None, act0, 0)
-
-    @pl.loop(0, pairs // 2 - 1)
+    for p in range(pairs):
+        step(acts[p % 2], p, acts[1 - p % 2] if p < pairs - 1 else None, p + 1)
+
+
+def predict(halves, w_mix, w_out, bias_out, total):
+    def mixed(i, g):
+        rows = slice(g * 16, (g + 1) * 16)
+        x = [ref[i, at : at + 8, rows, :].reshape(128, 256) for ref, at in halves]
+        x = jnp.concatenate(x, axis=0)
+        return jnp.dot(w_mix[g], x, preferred_element_type=F32) + x.astype(F32)
+
+    @pl.loop(0, 2)
     def _(k):
-        step(act0, 2 * k, act1, 2 * k + 1)
-        step(act1, 2 * k + 1, act0, 2 * k + 2)
-
-    step(act0, pairs - 2, act1, pairs - 1)
-    step(act1, pairs - 1, None, None)
-
-
-def predict(halves, w_mix, w_out, bias_out, total):
-    @pl.loop(0, 4)
-    def _(i):
-        def mixed(g):
-            rows = slice(g * 16, (g + 1) * 16)
-            x = [ref[i, at : at + 8, rows, :].reshape(128, 256) for ref, at in halves]
-            x = jnp.concatenate(x, axis=0)
-            return jnp.dot(w_mix[g], x, preferred_element_type=F32) + x.astype(F32)
-
-        acc = None
-        following = mixed(0)
-        for g in range(8):
+        order = [(2 * k + u, g) for u in range(2) for g in range(8)]
+        following = mixed(*order[0])
+        for n, (i, g) in enumerate(order):
             now = following
-            if g < 7:
-                following = mixed(g + 1)
+            if n < 15:
+                following = mixed(*order[n + 1])
             h = 0.5 * now
             outer = (h * jnp.tanh(h) + h).astype(BF16)
-            p = jnp.dot(w_out[g], outer, preferred_element_type=F32)
-            acc = p if acc is None else acc + p
-        for o in range(3):
-            part = acc[o * 16 : (o + 1) * 16, :] + bias_out[o]
-            for e in range(2):
-                total[2 * i + e, o * 16 : (o + 1) * 16, :] = part[:, e * 128 : (e + 1) * 128]
+            if g % 2 == 0:
+                held = outer
+                continue
+            w = jnp.concatenate([w_out[g - 1], w_out[g]], axis=1)
+            p = jnp.dot(w, jnp.concatenate([held, outer], axis=0), preferred_element_type=F32)
+            acc = p if g == 1 else acc + p
+            if g == 7:
+                for o in range(3):
+                    part = acc[o * 16 : (o + 1) * 16, :] + bias_out[o]
+                    for e in range(2):
+                        total[2 * i + e, o * 16 : (o + 1) * 16, :] = part[:, e * 128 : (e + 1) * 128]
 
 
 def unorder(total, maps, rows):
@@ -396,25 +406,25 @@
 ):
     n_t = lax.axis_size("tm")
     n_r = lax.axis_size("rows")
-    down = [(i, i + 1) for i in range(n_r - 1)]
-    up = [(i + 1, i) for i in range(n_r - 1)]
+    near = [(i, i ^ 1) for i in range(n_r)]
+    far = [(i, (i - 1 ^ 1) + 1) for i in range(1, n_r - 1)]
     back = [(i + 1, i) for i in range(n_t - 1)]
     forth = [(i, i + 1) for i in range(n_t - 1)]
     blend = blend_weight.T
     tile = shape((3, 16, 8, 128), BF16)
 
     raw = [noisy_frames, jnp.transpose(base_queue[:, :, 0, :], (1, 0, 2))]
-    to_below, to_above, base, own = call(
+    to_near, to_far, base, own = call(
         pack_kernel,
         "pack",
         [],
         raw,
-        (tile, tile, shape((48, 128), F32), tile),
+        (shape((144, 128), BF16), shape((144, 128), BF16), shape((48, 128), BF16), tile),
         [pltpu.VMEM((384, 128), F32)] + copies_of(raw)[1:],
         space=HBM,
     )
-    from_above = lax.ppermute(to_below, "rows", down)
-    from_below = lax.ppermute(to_above, "rows", up)
+    from_far = lax.ppermute(to_far, "rows", far)
+    from_near = lax.ppermute(to_near, "rows", near)
     raw = [
         jnp.asarray(tap_matrix(), BF16),
         weight_in.reshape(9, 6, 128),
@@ -442,7 +452,7 @@
     )
     rim, ask, pack = pl.pallas_call(
         middle_kernel,
-        out_shape=(tile, shape((n_t, 48, 128), BF16), shape((3, 8, 16, 128), BF16)),
+        out_shape=(tile, shape((n_t, 24, 128), BF16), shape((3, 8, 16, 128), BF16)),
         in_specs=[HBM] + [VMEM] * 5,
         out_specs=(VMEM,) * 3,
         scratch_shapes=[
@@ -452,7 +462,7 @@
         ],
         compiler_params=PARAMS,
         name="middle",
-    )(pltpu.with_memory_space_constraint(blend, pltpu.HBM), own, from_above, from_below, base, maps)
+    )(pltpu.with_memory_space_constraint(blend, pltpu.HBM), own, from_near, from_far, base, maps)
     queue = lax.all_to_all(ask, "tm", 0, 0, tiled=True)
     ahead = lax.ppermute(pack, "tm", back)
     gain = gain_mid.reshape(1, 128)
@@ -465,7 +475,7 @@
         network_scratch(16),
         flops=10**10,
     )
-    send, near = call(
+    send, next_half = call(
         late_kernel,
         "late",
         [frame_slot, bias_out],
@@ -479,7 +489,7 @@
         early_kernel,
         "early",
         [bias_out, blend],
-        [maps, w_mix, w_out, spatial, near],
+        [maps, w_mix, w_out, spatial, next_half],
         (shape((3, 16, 8, 128), F32),),
         PICTURES,
         flops=5 * 10**9,

time: 57.5 us -> 50.6 us (0.88)
  the two profiles are of different devices: /device:TPU:95 before, /device:TPU:160 now
where the time goes in v3:
time: 50.6 us; the launch traced here: 50.3 us
  Pallas kernels  28.1 us (56%)
  starting transfers between devices  18 us (36%)
  waiting for transfers between devices  4.07 us (8%)
    pallas_call x6, Pallas kernels, call(): pl.pallas_call(kernel, out_shape=outs, in_specs=[SMEM] * len(scalars) + [...  26.8 us
    all_to_all x1, starting transfers between devices, body(): queue = lax.all_to_all(ask, 'tm', 0, 0, tiled=True)  5.77 us
    ppermute x1, starting transfers between devices, body(): from_far = lax.ppermute(to_far, 'rows', far)  5 us
    ppermute x1, starting transfers between devices, body(): ahead = lax.ppermute(pack, 'tm', back)  4.57 us
    ppermute x1, starting transfers between devices, body(): arrived = lax.ppermute(send, 'tm', forth)  2.54 us
    ppermute x1, waiting for transfers between devices, body(): from_far = lax.ppermute(to_far, 'rows', far)  2.32 us
    ppermute x1, waiting for transfers between devices, body(): arrived = lax.ppermute(send, 'tm', forth)  1.4 us
    pallas_call x1, Pallas kernels, body(): pl.pallas_call(middle_kernel, out_shape=(tile, shape((n_t, 24, 128), BF16...  1.32 us
  transfers between devices with their start and end apart: 5, of which 3 were waited for; matrix products, arithmetic and copies ran while one was open for 0% of the time, Pallas kernels for 31%

profile of v3, /device:TPU:160, one launch (start us, length us, event | category | flops | bytes accessed | tf_op | source)
XLA Modules:
  0.0 50.3 jit_solution(8237052090139005635)
XLA Ops:
  0.0 0.0 copy-start.1
  0.0 0.0 copy-start.2
  0.0 1.1 %pack.1 = (bf16[144,128]{1,0:T(8,128)(2,1)S(1)}, bf16[144,128]{1,0:T(8,128)(2,1)S(1)}, bf16[48,128]{1,0:T(8,128)(2,1)S(1)}, bf16[3,16,8,128]{3,2,1,0:T(8,128)(2,1)S(1)}) custom-call(bf16[3,16,8,128]{3,2,1,0:T(8,128)(2,1)} %own_hbm.1, bf16[3,16,16]{2,1,0:T(8,128)(2,1)} %bitcast.17), custom_call_target="tpu_custom_call" | custom-call | flops 100000000 | bytes 1000000 | tf_op jit(solution)/shard_map/pack/pallas_call | solution.py:387
  1.1 0.1 collective-permute-start
  1.2 5.0 %collective-permute-start.1 = (bf16[144,128]{1,0:T(8,128)(2,1)S(1)}, bf16[144,128]{1,0:T(8,128)(2,1)S(1)}, u32[]{:S(2)}, u32[]{:S(2)}) collective-permute-start(bf16[144,128]{1,0:T(8,128)(2,1)S(1)} %get-tuple-element.24), channel_id=1, source_target_pairs={{1,2},{2,1},{3,4},{4,3},{5,6},{6,5},{7,8},{8,7},{9,10},{10,9},{11,... | collective-permute-start | bytes 110600 | tf_op jit(solution)/shard_map/ppermute | solution.py:426
  6.2 2.1 %prepare.1 = (bf16[5,256,256]{2,1,0:T(8,128)(2,1)S(1)}, bf16[256,1536]{1,0:T(8,128)(2,1)S(1)}, bf16[8,256,256]{2,1,0:T(8,128)(2,1)S(1)}, bf16[8,48,256]{2,1,0:T(8,128)(2,1)S(1)}, bf16[128,896]{1,0:T(8,128)(2,1)S(1)}) custom-call(bf16[10,256,72]{2,1,0:T(8,128)(2,1)} %constant.4.clone.refs_0_, bf16[9,6,128]{2,1,0:T(8,128)(2,1)} %bitcast.16, ...), custom_call_target="tpu_custom_call" | custom-call | flops 2000000000 | bytes 1000000 | tf_op jit(solution)/shard_map/prepare/pallas_call | solution.py:387
  8.4 0.0 collective-permute-done.near
  8.4 2.3 %collective-permute-done.1.far = bf16[144,128]{1,0:T(8,128)(2,1)S(1)} collective-permute-done((bf16[144,128]{1,0:T(8,128)(2,1)S(1)}, bf16[144,128]{1,0:T(8,128)(2,1)S(1)}, u32[]{:S(2)}, u32[]{:S(2)}) %collective-permute-start.1) | collective-permute-done | bytes 36896 | tf_op jit(solution)/shard_map/ppermute | solution.py:426
  10.7 1.3 %middle.1 = (bf16[3,16,8,128]{3,2,1,0:T(8,128)(2,1)S(1)}, bf16[8,24,128]{2,1,0:T(8,128)(2,1)}, bf16[3,8,16,128]{3,2,1,0:T(8,128)(2,1)S(1)}) custom-call(s32[2,16]{1,0:T(2,128)} %bitcast.10, bf16[3,16,8,128]{3,2,1,0:T(8,128)(2,1)S(1)} %get-tuple-element.22.own, bf16[144,128]{1,0:T(8,128)(2,1)S(1)} %collective-permute-done.near, ...), custom_call_target="tpu_custom_call" | custom-call | tf_op jit(solution)/shard_map/middle/pallas_call | solution.py:453
  12.0 5.8 %all-to-all-start = ((bf16[8,24,128]{2,1,0:T(8,128)(2,1)}), bf16[8,24,128]{2,1,0:T(8,128)(2,1)S(1)}, u32[]{:S(2)}, u32[]{:S(2)}) async-start(bf16[8,24,128]{2,1,0:T(8,128)(2,1)} %get-tuple-element.27), calls=%async_computation | async-start | bytes 98304 | tf_op jit(solution)/shard_map/all_to_all | solution.py:466
  17.8 4.6 %collective-permute-start.2 = (bf16[3,8,16,128]{3,2,1,0:T(8,128)(2,1)S(1)}, bf16[3,8,16,128]{3,2,1,0:T(8,128)(2,1)S(1)}, u32[]{:S(2)}, u32[]{:S(2)}) collective-permute-start(bf16[3,8,16,128]{3,2,1,0:T(8,128)(2,1)S(1)} %get-tuple-element.30), channel_id=1, source_target_pairs={{32,0},{64,32},{96,64},{128,96},{160,128},{192,160},{224,192},{33,... | collective-permute-start | bytes 294920 | tf_op jit(solution)/shard_map/ppermute | solution.py:467
  22.4 0.3 all-to-all-done.queue
  22.7 0.0 copy-done.1
  22.7 0.0 copy-done.2
  22.7 0.0 copy-start.3
  22.7 9.5 %own.1 = bf16[4,16,128,256]{3,2,1,0:T(8,128)(2,1)S(1)} custom-call(s32[128]{0:T(128)S(1)} %copy-done.1, bf16[3,16,8,128]{3,2,1,0:T(8,128)(2,1)S(1)} %get-tuple-element.22.own, bf16[3,16,8,128]{3,2,1,0:T(8,128)(2,1)S(1)} %get-tuple-element.26.rim, bf16[8,24,128]{2,1,0:T(8,128)(2,1)S(1)} %all-to-all-done.queue, f32[1,128]{1,0:T(1,128)S(1)} %bitcast.12, ...), custom_call_target="tpu_custom_call" | custom-call | flops 10000000000 | bytes 1000000 | tf_op jit(solution)/shard_map/own/pallas_call | solution.py:387
  32.3 0.0 collective-permute-done.2.ahead
  32.3 0.0 copy-done.3
  32.3 0.0 copy-start
  32.3 9.2 %late.1 = (bf16[3,8,8,128]{3,2,1,0:T(8,128)(2,1)S(1)}, f32[3,8,8,128]{3,2,1,0:T(8,128)S(1)}) custom-call(s32[128]{0:T(128)S(1)} %copy-done.1, f32[3]{0:T(128)S(1)} %copy-done.3, bf16[3,8,16,128]{3,2,1,0:T(8,128)(2,1)S(1)} %collective-permute-done.2.ahead, bf16[8,24,128]{2,1,0:T(8,128)(2,1)S(1)} %all-to-all-done.queue, f32[1,128]{1,0:T(1,128)S(1)} %bitcast.13, ...), custom_call_target="tpu_custom_call" | custom-call | flops 10000000000 | bytes 1000000 | tf_op jit(solution)/shard_map/late/pallas_call | solution.py:387
  41.5 2.5 %collective-permute-start.3 = (bf16[3,8,8,128]{3,2,1,0:T(8,128)(2,1)S(1)}, bf16[3,8,8,128]{3,2,1,0:T(8,128)(2,1)S(1)}, u32[]{:S(2)}, u32[]{:S(2)}) collective-permute-start(bf16[3,8,8,128]{3,2,1,0:T(8,128)(2,1)S(1)} %get-tuple-element.32), channel_id=1, source_target_pairs={{0,32},{32,64},{64,96},{96,128},{128,160},{160,192},{192,224},{1,3... | collective-permute-start | bytes 147464 | tf_op jit(solution)/shard_map/ppermute | solution.py:487
  44.0 0.0 copy-done
  44.0 4.1 %early.1.mine = f32[3,16,8,128]{3,2,1,0:T(8,128)S(1)} custom-call(f32[3]{0:T(128)S(1)} %copy-done.3, s32[2,16]{1,0:T(2,128)S(1)} %bitcast.11, bf16[128,896]{1,0:T(8,128)(2,1)S(1)} %get-tuple-element.19.maps, bf16[8,256,256]{2,1,0:T(8,128)(2,1)S(1)} %get-tuple-element.20.w_mix, bf16[8,48,256]{2,1,0:T(8,128)(2,1)S(1)} %get-tuple-element.21.w_out, ...), custom_call_target="tpu_custom_call" | custom-call | flops 5000000000 | bytes 1000000 | tf_op jit(solution)/shard_map/early/pallas_call | solution.py:387
  48.2 1.4 %collective-permute-done.3.arrived = bf16[3,8,8,128]{3,2,1,0:T(8,128)(2,1)S(1)} collective-permute-done((bf16[3,8,8,128]{3,2,1,0:T(8,128)(2,1)S(1)}, bf16[3,8,8,128]{3,2,1,0:T(8,128)(2,1)S(1)}, u32[]{:S(2)}, u32[]{:S(2)}) %collective-permute-start.3) | collective-permute-done | bytes 49184 | tf_op jit(solution)/shard_map/ppermute | solution.py:487
  49.6 0.7 %join.1 = f32[3,16,8,128]{3,2,1,0:T(8,128)} custom-call(f32[3,16,8,128]{3,2,1,0:T(8,128)S(1)} %early.1.mine, bf16[3,8,8,128]{3,2,1,0:T(8,128)(2,1)S(1)} %collective-permute-done.3.arrived), custom_call_target="tpu_custom_call" | custom-call | flops 100000000 | bytes 1000000 | tf_op jit(solution)/shard_map/join/pallas_call | solution.py:387
Async XLA Ops:
  0.0 22.7 %copy-start.1 = (s32[128]{0:T(128)S(1)}, s32[128]{0:T(128)}, u32[]{:S(2)}) copy-start(s32[128]{0:T(128)} %frame_slot.3) | copy-start | bytes 1540
  0.0 22.7 %copy-start.2 = (f32[128]{0:T(128)S(1)}, f32[128]{0:T(128)}, u32[]{:S(2)}) copy-start(f32[128]{0:T(128)} %param.19) | copy-start | bytes 1540
  1.1 7.3 %collective-permute-start = (bf16[144,128]{1,0:T(8,128)(2,1)S(1)}, bf16[144,128]{1,0:T(8,128)(2,1)S(1)}, u32[]{:S(2)}, u32[]{:S(2)}) collective-permute-start(bf16[144,128]{1,0:T(8,128)(2,1)S(1)} %get-tuple-element.23), channel_id=1, source_target_pairs={{0,1},{1,0},{2,3},{3,2},{4,5},{5,4},{6,7},{7,6},{8,9},{9,8},{10,11... | collective-permute-start | bytes 110600 | tf_op jit(solution)/shard_map/ppermute | solution.py:427
  1.2 9.5 %collective-permute-start.1 = (bf16[144,128]{1,0:T(8,128)(2,1)S(1)}, bf16[144,128]{1,0:T(8,128)(2,1)S(1)}, u32[]{:S(2)}, u32[]{:S(2)}) collective-permute-start(bf16[144,128]{1,0:T(8,128)(2,1)S(1)} %get-tuple-element.24), channel_id=1, source_target_pairs={{1,2},{2,1},{3,4},{4,3},{5,6},{6,5},{7,8},{8,7},{9,10},{10,9},{11,... | collective-permute-start | bytes 110600 | tf_op jit(solution)/shard_map/ppermute | solution.py:426
  12.0 10.7 %all-to-all-start = ((bf16[8,24,128]{2,1,0:T(8,128)(2,1)}), bf16[8,24,128]{2,1,0:T(8,128)(2,1)S(1)}, u32[]{:S(2)}, u32[]{:S(2)}) async-start(bf16[8,24,128]{2,1,0:T(8,128)(2,1)} %get-tuple-element.27), calls=%async_computation | async-start | bytes 98304 | tf_op jit(solution)/shard_map/all_to_all | solution.py:466
  17.8 14.5 %collective-permute-start.2 = (bf16[3,8,16,128]{3,2,1,0:T(8,128)(2,1)S(1)}, bf16[3,8,16,128]{3,2,1,0:T(8,128)(2,1)S(1)}, u32[]{:S(2)}, u32[]{:S(2)}) collective-permute-start(bf16[3,8,16,128]{3,2,1,0:T(8,128)(2,1)S(1)} %get-tuple-element.30), channel_id=1, source_target_pairs={{32,0},{64,32},{96,64},{128,96},{160,128},{192,160},{224,192},{33,... | collective-permute-start | bytes 294920 | tf_op jit(solution)/shard_map/ppermute | solution.py:467
  22.7 9.6 %copy-start.3 = (f32[3]{0:T(128)S(1)}, f32[3]{0:T(128)}, u32[]{:S(2)}) copy-start(f32[3]{0:T(128)} %bias_out.3) | copy-start | bytes 40
  32.3 11.8 %copy-start = (s32[16,2]{0,1:T(2,128)S(1)}, s32[16,2]{0,1:T(2,128)}, u32[]{:S(2)}) copy-start(s32[16,2]{0,1:T(2,128)} %param.16) | copy-start | bytes 388
  41.5 8.1 %collective-permute-start.3 = (bf16[3,8,8,128]{3,2,1,0:T(8,128)(2,1)S(1)}, bf16[3,8,8,128]{3,2,1,0:T(8,128)(2,1)S(1)}, u32[]{:S(2)}, u32[]{:S(2)}) collective-permute-start(bf16[3,8,8,128]{3,2,1,0:T(8,128)(2,1)S(1)} %get-tuple-element.32), channel_id=1, source_target_pairs={{0,32},{32,64},{64,96},{96,128},{128,160},{160,192},{192,224},{1,3... | collective-permute-start | bytes 147464 | tf_op jit(solution)/shard_map/ppermute | solution.py:487

commit v4 on v3

--- a/solution.py
+++ b/solution.py
@@ -77,11 +77,7 @@
     base[...] = placed[:, 128:256].astype(BF16)
 
 
-def middle_kernel(
-    blend_hbm, own, near, far, base, maps, rim, ask, back, both, blend, sems
-):
-    copy = pltpu.make_async_copy(blend_hbm, blend, sems.at[0])
-    copy.start()
+def middle_kernel(own, near, far, base, weights, rim, ask, back, both):
     both[...] = jnp.zeros_like(both)
     even = lax.rem(lax.axis_index("rows"), 2) == 0
     for k in range(2):
@@ -96,21 +92,54 @@
     three = (three[:24] + pltpu.roll(three[24:], 64, 1)).astype(BF16)
     for i in range(ask.shape[0]):
         ask[i] = three
-    copy.wait()
     row = iota((8, 128), 0)
     for ch in range(3):
         for f in range(8):
-            y = x[ch, f]
-            y = jnp.where(row == 6, blend[0, f].astype(F32), y)
-            y = jnp.where(row == 7, blend[1, f].astype(F32), y)
+            y = jnp.where(row == 6, weights[f : f + 1, :], x[ch, f])
+            y = jnp.where(row == 7, weights[f + 8 : f + 9, :], y)
             both_rows = jnp.concatenate([own[ch, f].astype(F32), y], axis=0)
             back[ch, f] = both_rows.astype(BF16)
 
 
+def selection(frame_slot):
+    j = iota((8, 384), 0)
+    lane = iota((8, 384), 1)
+    start = lax.axis_index("tm") * 16
+    hot = []
+    for f in range(24):
+        slot = frame_slot[jnp.minimum(start + f, 127)]
+        row = j % 3 * 16 + slot % 16
+        place = slot // 16 * 24 + jnp.where(row < 24, row, row + 168)
+        hot.append(jnp.where((lane == place) & (j < 6), 1.0, 0.0))
+    return jnp.concatenate(hot, axis=0).astype(BF16)
+
+
+def blend_shares(blend):
+    t = lax.axis_index("tm")
+    has_prev = jnp.where(t > 0, 1.0, 0.0)
+    has_next = jnp.where(t < lax.axis_size("tm") - 1, 1.0, 0.0)
+    row = iota((16, 128), 0)
+    lead = jnp.zeros((16, 128), F32)
+    trail = jnp.zeros((16, 128), F32)
+    for f in range(16):
+        lead = jnp.where(row == f, blend[0, f].astype(F32), lead)
+        trail = jnp.where(row == f, blend[1, f].astype(F32), trail)
+    raw = jnp.concatenate([lead[0:8], trail[0:8]], axis=0)
+    lead = jnp.where(row < 8, lead, lead * has_next)
+    trail = jnp.where(row < 8, trail * has_prev, trail)
+    total = lead + trail
+    return raw, jnp.concatenate([lead / total, trail / total], axis=0)
+
+
 def prepare_kernel(*refs):
-    sources, (w_in, w_mid, w_mix, w_out, maps), targets = refs[:7], refs[7:12], refs[12:19]
-    fetch(sources, targets, refs[19])
-    taps, win, bias, wmid, mix, wout, over = targets
+    sources, made, targets, sems = refs[:10], refs[10:19], refs[19:29], refs[29]
+    fetch(sources, targets, sems)
+    taps, win, bias, wmid, mix, wout, over, blend, frame_slot, bias_out = targets
+    w_in, w_mid, w_mix, w_out, maps, weights, shares, hot, offset = made
+    weights[...], shares[...] = blend_shares(blend)
+    hot[...] = selection(frame_slot)
+    for o in range(3):
+        offset[o * 16 : (o + 1) * 16, :] = jnp.zeros((16, 128), F32) + bias_out[o]
     col = iota((128, 384), 0)
     lane = iota((128, 384), 1)
     pixel = lane & 127
@@ -159,20 +188,10 @@
             w_out[g, o * 16 : (o + 1) * 16, :] = jnp.where(own, t[o : o + 1, :], 0.0).astype(BF16)
 
 
-def lift(frame_slot, queue, maps, first, count):
-    j = iota((8, 384), 0)
-    lane = iota((8, 384), 1)
-    start = lax.axis_index("tm") * 16 + first
-    hot = []
-    for f in range(count):
-        slot = frame_slot[jnp.minimum(start + f, 127)]
-        row = j % 3 * 16 + slot % 16
-        place = slot // 16 * 24 + jnp.where(row < 24, row, row + 168)
-        hot.append(jnp.where((lane == place) & (j < 6), 1.0, 0.0))
-    hot = jnp.concatenate(hot, axis=0).astype(BF16)
+def lift(hot, queue, maps):
     rows = queue[...].astype(F32).reshape(192, 128)
     rows = jnp.concatenate([rows, pltpu.roll(rows, 64, 1)], axis=0).astype(BF16)
-    chosen = jnp.dot(hot, rows, preferred_element_type=F32).astype(BF16)
+    chosen = jnp.dot(hot[...], rows, preferred_element_type=F32).astype(BF16)
     return jnp.dot(chosen, maps[:, 384:768], preferred_element_type=F32)
 
 
@@ -245,7 +264,7 @@
             ]
 
 
-def network(inputs, pairs, w_in, w_mid, gain, act0, act1, spatial):
+def network(inputs, pairs, frame, maps, w_in, w_mid, gain, act0, act1, spatial):
     def step(done, pair, todo, following):
         if todo is not None:
             depth = spread_inputs(inputs, following)
@@ -259,40 +278,38 @@
                     h = jnp.dot(depth, w_in[q + 1], preferred_element_type=F32)
                 norm_act(now, gain[q], todo, q)
 
+    for part in range(pairs // 2):
+        stage(inputs, part * 4, [frame(part * 4 + f) for f in range(4)], maps)
     acts = [act0, act1]
     step(None, None, act0, 0)
     for p in range(pairs):
         step(acts[p % 2], p, acts[1 - p % 2] if p < pairs - 1 else None, p + 1)
 
 
-def predict(halves, w_mix, w_out, bias_out, total):
+def predict(halves, w_mix, w_out, offset, total):
     def mixed(i, g):
         rows = slice(g * 16, (g + 1) * 16)
         x = [ref[i, at : at + 8, rows, :].reshape(128, 256) for ref, at in halves]
         x = jnp.concatenate(x, axis=0)
         return jnp.dot(w_mix[g], x, preferred_element_type=F32) + x.astype(F32)
 
-    @pl.loop(0, 2)
-    def _(k):
-        order = [(2 * k + u, g) for u in range(2) for g in range(8)]
-        following = mixed(*order[0])
-        for n, (i, g) in enumerate(order):
-            now = following
-            if n < 15:
-                following = mixed(*order[n + 1])
-            h = 0.5 * now
-            outer = (h * jnp.tanh(h) + h).astype(BF16)
-            if g % 2 == 0:
-                held = outer
-                continue
-            w = jnp.concatenate([w_out[g - 1], w_out[g]], axis=1)
-            p = jnp.dot(w, jnp.concatenate([held, outer], axis=0), preferred_element_type=F32)
-            acc = p if g == 1 else acc + p
-            if g == 7:
-                for o in range(3):
-                    part = acc[o * 16 : (o + 1) * 16, :] + bias_out[o]
-                    for e in range(2):
-                        total[2 * i + e, o * 16 : (o + 1) * 16, :] = part[:, e * 128 : (e + 1) * 128]
+    order = [(i, g) for i in range(4) for g in range(8)]
+    queued = [mixed(*order[n]) for n in range(3)]
+    for n, (i, g) in enumerate(order):
+        now = queued.pop(0)
+        if n + 3 < len(order):
+            queued.append(mixed(*order[n + 3]))
+        h = 0.5 * now
+        outer = (h * jnp.tanh(h) + h).astype(BF16)
+        if g % 2 == 0:
+            held = outer
+            continue
+        w = jnp.concatenate([w_out[g - 1], w_out[g]], axis=1)
+        p = jnp.dot(w, jnp.concatenate([held, outer], axis=0), preferred_element_type=F32)
+        acc = p if g == 1 else acc + p
+        if g == 7:
+            for e in range(2):
+                total[2 * i + e] = acc[:, e * 128 : (e + 1) * 128] + offset[...]
 
 
 def unorder(total, maps, rows):
@@ -310,34 +327,30 @@
 
 
 def own_kernel(
-    frame_slot, own, rim, queue, gain, w_in, w_mid, maps, spatial, inputs, act0, act1
+    hot, own, rim, queue, gain, w_in, w_mid, maps, spatial, lifted_ahead, inputs, act0, act1
 ):
-    lifted = lift(frame_slot, queue, maps, 0, 16)
-    for part in range(4):
-        frames = []
-        for f in range(part * 4, part * 4 + 4):
-            noisy = [own[ch, f].astype(F32) for ch in range(3)]
-            edge = [rim[ch, f].astype(F32) for ch in range(3)]
-            frames.append(tiles_of(noisy, edge, lifted[f * 8 : f * 8 + 8]))
-        stage(inputs, part * 4, frames, maps)
-    network(inputs, 8, w_in, w_mid, gains(gain), act0, act1, spatial)
+    lifted = lift(hot, queue, maps)
+    lifted_ahead[...] = lifted[128:]
+
+    def frame(f):
+        noisy = [own[ch, f].astype(F32) for ch in range(3)]
+        edge = [rim[ch, f].astype(F32) for ch in range(3)]
+        return tiles_of(noisy, edge, lifted[f * 8 : f * 8 + 8])
+
+    network(inputs, 8, frame, maps, w_in, w_mid, gains(gain), act0, act1, spatial)
 
 
 def late_kernel(
-    frame_slot, bias_out, ahead, queue, gain, w_in, w_mid, maps, w_mix, w_out, own,
+    offset, ahead, lifted, gain, w_in, w_mid, maps, w_mix, w_out, own,
     send, near, inputs, act0, act1, spatial, total, rows,
 ):
-    lifted = lift(frame_slot, queue, maps, 16, 8)
-    for part in range(2):
-        frames = []
-        for f in range(part * 4, part * 4 + 4):
-            x = [ahead[ch, f].astype(F32) for ch in range(3)]
-            frames.append(
-                tiles_of([tile[:8] for tile in x], [tile[8:] for tile in x], lifted[f * 8 : f * 8 + 8])
-            )
-        stage(inputs, part * 4, frames, maps)
-    network(inputs, 4, w_in, w_mid, gains(gain), act0, act1, spatial)
-    predict([(own, 8), (spatial, 0)], w_mix, w_out, bias_out, total)
+    def frame(f):
+        x = [ahead[ch, f].astype(F32) for ch in range(3)]
+        noisy, edge = [tile[:8] for tile in x], [tile[8:] for tile in x]
+        return tiles_of(noisy, edge, lifted[f * 8 : f * 8 + 8, :])
+
+    network(inputs, 4, frame, maps, w_in, w_mid, gains(gain), act0, act1, spatial)
+    predict([(own, 8), (spatial, 0)], w_mix, w_out, offset, total)
     unorder(total, maps, rows)
     for f in range(8):
         w = ahead[0, f].astype(F32)
@@ -347,21 +360,16 @@
             send[o, f] = (picture(rows, o, f + 8) * share).astype(BF16)
 
 
-def early_kernel(bias_out, blend, maps, w_mix, w_out, own, near, mine, total, rows):
-    predict([(own, 0), (own, 8)], w_mix, w_out, bias_out, total)
+def early_kernel(offset, shares, maps, w_mix, w_out, own, near, mine, total, rows):
+    predict([(own, 0), (own, 8)], w_mix, w_out, offset, total)
     unorder(total, maps, rows)
-    t = lax.axis_index("tm")
-    has_prev = jnp.where(t > 0, 1.0, 0.0)
-    has_next = jnp.where(t < lax.axis_size("tm") - 1, 1.0, 0.0)
-    one = jnp.ones((8, 128), F32)
-    for f in range(8):
-        lead = one * blend[0, f].astype(F32)
-        share = lead / (lead + one * (blend[1, f].astype(F32) * has_prev))
-        lead = one * (blend[0, f + 8].astype(F32) * has_next)
-        trail = one * blend[1, f + 8].astype(F32)
+    for f in range(16):
+        lead, trail = shares[f : f + 1, :], shares[f + 16 : f + 17, :]
         for o in range(3):
-            mine[o, f] = picture(rows, o, f) * share
-            mine[o, f + 8] = (lead * near[o, f] + trail * picture(rows, o, f + 8)) / (lead + trail)
+            if f < 8:
+                mine[o, f] = picture(rows, o, f) * lead
+            else:
+                mine[o, f] = near[o, f - 8] * lead + picture(rows, o, f) * trail
 
 
 def join_kernel(mine, arrived, out):
@@ -433,8 +441,11 @@
         jnp.transpose(time_mix, (1, 2, 0)),
         weight_out.T,
         jnp.asarray(spread_matrix(), BF16),
+        blend,
+        frame_slot,
+        bias_out,
     ]
-    w_in, w_mid, w_mix, w_out, maps = call(
+    w_in, w_mid, w_mix, w_out, maps, weights, shares, hot, offset = call(
         prepare_kernel,
         "prepare",
         [],
@@ -445,41 +456,43 @@
             shape((8, 256, 256), BF16),
             shape((8, 48, 256), BF16),
             shape((128, 896), BF16),
+            shape((16, 128), F32),
+            shape((32, 128), F32),
+            shape((192, 384), BF16),
+            shape((48, 128), F32),
         ),
-        copies_of(raw),
+        copies_of(raw[:7])[:7]
+        + [pltpu.SMEM(a.shape, a.dtype) for a in raw[7:]]
+        + [pltpu.SemaphoreType.DMA((10,))],
         flops=2 * 10**9,
         space=HBM,
     )
     rim, ask, pack = pl.pallas_call(
         middle_kernel,
         out_shape=(tile, shape((n_t, 24, 128), BF16), shape((3, 8, 16, 128), BF16)),
-        in_specs=[HBM] + [VMEM] * 5,
+        in_specs=[VMEM] * 5,
         out_specs=(VMEM,) * 3,
-        scratch_shapes=[
-            pltpu.VMEM((384, 128), F32),
-            pltpu.SMEM((2, 16), jnp.int32),
-            pltpu.SemaphoreType.DMA((1,)),
-        ],
+        scratch_shapes=[pltpu.VMEM((384, 128), F32)],
         compiler_params=PARAMS,
         name="middle",
-    )(pltpu.with_memory_space_constraint(blend, pltpu.HBM), own, from_near, from_far, base, maps)
+    )(own, from_near, from_far, base, weights)
     queue = lax.all_to_all(ask, "tm", 0, 0, tiled=True)
     ahead = lax.ppermute(pack, "tm", back)
     gain = gain_mid.reshape(1, 128)
-    (spatial,) = call(
+    spatial, lifted_ahead = call(
         own_kernel,
         "own",
-        [frame_slot],
-        [own, rim, queue, gain, w_in, w_mid, maps],
-        (shape((4, 16, 128, 256), BF16),),
+        [],
+        [hot, own, rim, queue, gain, w_in, w_mid, maps],
+        (shape((4, 16, 128, 256), BF16), shape((64, 384), F32)),
         network_scratch(16),
         flops=10**10,
     )
     send, next_half = call(
         late_kernel,
         "late",
-        [frame_slot, bias_out],
-        [ahead, queue, gain, w_in, w_mid, maps, w_mix, w_out, spatial],
+        [],
+        [offset, ahead, lifted_ahead, gain, w_in, w_mid, maps, w_mix, w_out, spatial],
         (shape((3, 8, 8, 128), BF16), shape((3, 8, 8, 128), F32)),
         network_scratch(8) + [pltpu.VMEM((4, 8, 128, 256), BF16)] + PICTURES,
         flops=10**10,
@@ -488,8 +501,8 @@
     (mine,) = call(
         early_kernel,
         "early",
-        [bias_out, blend],
-        [maps, w_mix, w_out, spatial, next_half],
+        [],
+        [offset, shares, maps, w_mix, w_out, spatial, next_half],
         (shape((3, 16, 8, 128), F32),),
         PICTURES,
         flops=5 * 10**9,

time: 50.6 us -> 49.1 us (0.970)
  Pallas kernels: 28.1 us -> 26 us
  waiting for transfers between devices: 4.07 us -> 4.73 us
    pallas_call x6, Pallas kernels: 26.8 us -> 25.3 us  [call(): pl.pallas_call(kernel, out_shape=outs, in_specs=[SMEM] * len(scalars) + [...]
    ppermute x1, waiting for transfers between devices: 1.4 us -> 2.23 us  [body(): arrived = lax.ppermute(send, 'tm', forth)]
    pallas_call x1, Pallas kernels: 1.32 us -> 0.7 us  [body(): pl.pallas_call(middle_kernel, out_shape=(tile, shape((n_t, 24, 128), BF16...]
where the time goes in v4:
time: 49.1 us; the launch traced here: 48.8 us
  Pallas kernels  26 us (53%)
  starting transfers between devices  18 us (37%)
  waiting for transfers between devices  4.73 us (10%)
    pallas_call x6, Pallas kernels, call(): pl.pallas_call(kernel, out_shape=outs, in_specs=[SMEM] * len(scalars) + [...  25.3 us
    all_to_all x1, starting transfers between devices, body(): queue = lax.all_to_all(ask, 'tm', 0, 0, tiled=True)  5.76 us
    ppermute x1, starting transfers between devices, body(): from_far = lax.ppermute(to_far, 'rows', far)  5 us
    ppermute x1, starting transfers between devices, body(): ahead = lax.ppermute(pack, 'tm', back)  4.57 us
    ppermute x1, starting transfers between devices, body(): arrived = lax.ppermute(send, 'tm', forth)  2.53 us
    ppermute x1, waiting for transfers between devices, body(): arrived = lax.ppermute(send, 'tm', forth)  2.23 us
    ppermute x1, waiting for transfers between devices, body(): from_far = lax.ppermute(to_far, 'rows', far)  2.17 us
  transfers between devices with their start and end apart: 5, of which 3 were waited for; matrix products, arithmetic and copies ran while one was open for 0% of the time, Pallas kernels for 31%

profile of v4, /device:TPU:160, one launch (start us, length us, event | category | flops | bytes accessed | tf_op | source)
XLA Modules:
  0.0 48.8 jit_solution(10146961118102717689)
XLA Ops:
  0.0 0.0 copy-start
  0.0 1.1 %pack.1 = (bf16[144,128]{1,0:T(8,128)(2,1)S(1)}, bf16[144,128]{1,0:T(8,128)(2,1)S(1)}, bf16[48,128]{1,0:T(8,128)(2,1)S(1)}, bf16[3,16,8,128]{3,2,1,0:T(8,128)(2,1)S(1)}) custom-call(bf16[3,16,8,128]{3,2,1,0:T(8,128)(2,1)} %own_hbm.1, bf16[3,16,16]{2,1,0:T(8,128)(2,1)} %bitcast.15), custom_call_target="tpu_custom_call" | custom-call | flops 100000000 | bytes 1000000 | tf_op jit(solution)/shard_map/pack/pallas_call | solution.py:395
  1.1 0.1 collective-permute-start
  1.2 5.0 %collective-permute-start.1 = (bf16[144,128]{1,0:T(8,128)(2,1)S(1)}, bf16[144,128]{1,0:T(8,128)(2,1)S(1)}, u32[]{:S(2)}, u32[]{:S(2)}) collective-permute-start(bf16[144,128]{1,0:T(8,128)(2,1)S(1)} %get-tuple-element.33), channel_id=1, source_target_pairs={{1,2},{2,1},{3,4},{4,3},{5,6},{6,5},{7,8},{8,7},{9,10},{10,9},{11,... | collective-permute-start | bytes 110600 | tf_op jit(solution)/shard_map/ppermute | solution.py:434
  6.2 2.3 %prepare.1 = (bf16[5,256,256]{2,1,0:T(8,128)(2,1)S(1)}, bf16[256,1536]{1,0:T(8,128)(2,1)S(1)}, bf16[8,256,256]{2,1,0:T(8,128)(2,1)S(1)}, bf16[8,48,256]{2,1,0:T(...) custom-call(bf16[10,256,72]{2,1,0:T(8,128)(2,1)} %constant.4.clone.r, ...), custom_call_target="tpu_custom_call" | custom-call | flops 2000000000 | bytes 1000000 | tf_op jit(solution)/shard_map/prepare/pallas_call | solution.py:395
  8.5 0.0 collective-permute-done.near
  8.5 2.2 %collective-permute-done.1.far = bf16[144,128]{1,0:T(8,128)(2,1)S(1)} collective-permute-done((bf16[144,128]{1,0:T(8,128)(2,1)S(1)}, bf16[144,128]{1,0:T(8,128)(2,1)S(1)}, u32[]{:S(2)}, u32[]{:S(2)}) %collective-permute-start.1) | collective-permute-done | bytes 36896 | tf_op jit(solution)/shard_map/ppermute | solution.py:434
  10.7 0.7 %middle.1 = (bf16[3,16,8,128]{3,2,1,0:T(8,128)(2,1)S(1)}, bf16[8,24,128]{2,1,0:T(8,128)(2,1)}, bf16[3,8,16,128]{3,2,1,0:T(8,128)(2,1)S(1)}) custom-call(bf16[3,16,8,128]{3,2,1,0:T(8,128)(2,1)S(1)} %get-tuple-element.31.own, bf16[144,128]{1,0:T(8,128)(2,1)S(1)} %collective-permute-done.near, bf16[144,128]{1,0:T(8,128)(2,1)S(1)} %collective-permute-done.1.far, ...), custom_call_target="tpu_custom_call" | custom-call | tf_op jit(solution)/shard_map/middle/pallas_call | solution.py:470
  11.4 5.8 %all-to-all-start = ((bf16[8,24,128]{2,1,0:T(8,128)(2,1)}), bf16[8,24,128]{2,1,0:T(8,128)(2,1)S(1)}, u32[]{:S(2)}, u32[]{:S(2)}) async-start(bf16[8,24,128]{2,1,0:T(8,128)(2,1)} %get-tuple-element.37), calls=%async_computation | async-start | bytes 98304 | tf_op jit(solution)/shard_map/all_to_all | solution.py:479
  17.1 4.6 %collective-permute-start.2 = (bf16[3,8,16,128]{3,2,1,0:T(8,128)(2,1)S(1)}, bf16[3,8,16,128]{3,2,1,0:T(8,128)(2,1)S(1)}, u32[]{:S(2)}, u32[]{:S(2)}) collective-permute-start(bf16[3,8,16,128]{3,2,1,0:T(8,128)(2,1)S(1)} %get-tuple-element.41), channel_id=1, source_target_pairs={{32,0},{64,32},{96,64},{128,96},{160,128},{192,160},{224,192},{33,... | collective-permute-start | bytes 294920 | tf_op jit(solution)/shard_map/ppermute | solution.py:480
  21.7 0.3 all-to-all-done.queue
  22.0 0.0 copy-done
  22.0 9.6 %own.1 = (bf16[4,16,128,256]{3,2,1,0:T(8,128)(2,1)S(1)}, f32[64,384]{1,0:T(8,128)S(1)}) custom-call(bf16[192,384]{1,0:T(8,128)(2,1)S(1)} %get-tuple-element.30.hot, bf16[3,16,8,128]{3,2,1,0:T(8,128)(2,1)S(1)} %get-tuple-element.31.own, bf16[3,16,8,128]{3,2,1,0:T(8,128)(2,1)S(1)} %get-tuple-element.36.rim, bf16[8,24,128]{2,1,0:T(8,128)(2,1)S(1)} %all-to-all-done.queue, ...), custom_call_target="tpu_custom_call" | custom-call | flops 10000000000 | bytes 1000000 | tf_op jit(solution)/shard_map/own/pallas_call | solution.py:395
  31.7 0.0 collective-permute-done.2.ahead
  31.7 8.4 %late.1 = (bf16[3,8,8,128]{3,2,1,0:T(8,128)(2,1)S(1)}, f32[3,8,8,128]{3,2,1,0:T(8,128)S(1)}) custom-call(f32[48,128]{1,0:T(8,128)S(1)} %get-tuple-element.25.offset, bf16[3,8,16,128]{3,2,1,0:T(8,128)(2,1)S(1)} %collective-permute-done.2.ahead, f32[64,384]{1,0:T(8,128)S(1)} %get-tuple-element.42.lifted, f32[1,128]{1,0:T(1,128)S(1)} %bitcast.11, ...), custom_call_target="tpu_custom_call" | custom-call | flops 10000000000 | bytes 1000000 | tf_op jit(solution)/shard_map/late/pallas_call | solution.py:395
  40.0 2.5 %collective-permute-start.3 = (bf16[3,8,8,128]{3,2,1,0:T(8,128)(2,1)S(1)}, bf16[3,8,8,128]{3,2,1,0:T(8,128)(2,1)S(1)}, u32[]{:S(2)}, u32[]{:S(2)}) collective-permute-start(bf16[3,8,8,128]{3,2,1,0:T(8,128)(2,1)S(1)} %get-tuple-element.44), channel_id=1, source_target_pairs={{0,32},{32,64},{64,96},{96,128},{128,160},{160,192},{192,224},{1,3... | collective-permute-start | bytes 147464 | tf_op jit(solution)/shard_map/ppermute | solution.py:500
  42.6 3.3 %early.1.mine = f32[3,16,8,128]{3,2,1,0:T(8,128)S(1)} custom-call(f32[48,128]{1,0:T(8,128)S(1)} %get-tuple-element.25.offset, f32[32,128]{1,0:T(8,128)S(1)} %get-tuple-element.26.shares, bf16[128,896]{1,0:T(8,128)(2,1)S(1)} %get-tuple-element.27.maps, bf16[8,256,256]{2,1,0:T(8,128)(2,1)S(1)} %get-tuple-element.28.w_mix, ...), custom_call_target="tpu_custom_call" | custom-call | flops 5000000000 | bytes 1000000 | tf_op jit(solution)/shard_map/early/pallas_call | solution.py:395
  45.9 2.2 %collective-permute-done.3.arrived = bf16[3,8,8,128]{3,2,1,0:T(8,128)(2,1)S(1)} collective-permute-done((bf16[3,8,8,128]{3,2,1,0:T(8,128)(2,1)S(1)}, bf16[3,8,8,128]{3,2,1,0:T(8,128)(2,1)S(1)}, u32[]{:S(2)}, u32[]{:S(2)}) %collective-permute-start.3) | collective-permute-done | bytes 49184 | tf_op jit(solution)/shard_map/ppermute | solution.py:500
  48.1 0.7 %join.1 = f32[3,16,8,128]{3,2,1,0:T(8,128)} custom-call(f32[3,16,8,128]{3,2,1,0:T(8,128)S(1)} %early.1.mine, bf16[3,8,8,128]{3,2,1,0:T(8,128)(2,1)S(1)} %collective-permute-done.3.arrived), custom_call_target="tpu_custom_call" | custom-call | flops 100000000 | bytes 1000000 | tf_op jit(solution)/shard_map/join/pallas_call | solution.py:395
Async XLA Ops:
  0.0 22.0 %copy-start = (f32[128]{0:T(128)S(1)}, f32[128]{0:T(128)}, u32[]{:S(2)}) copy-start(f32[128]{0:T(128)} %param.19) | copy-start | bytes 1540
  1.1 7.4 %collective-permute-start = (bf16[144,128]{1,0:T(8,128)(2,1)S(1)}, bf16[144,128]{1,0:T(8,128)(2,1)S(1)}, u32[]{:S(2)}, u32[]{:S(2)}) collective-permute-start(bf16[144,128]{1,0:T(8,128)(2,1)S(1)} %get-tuple-element.32), channel_id=1, source_target_pairs={{0,1},{1,0},{2,3},{3,2},{4,5},{5,4},{6,7},{7,6},{8,9},{9,8},{10,11... | collective-permute-start | bytes 110600 | tf_op jit(solution)/shard_map/ppermute | solution.py:435
  1.2 9.5 %collective-permute-start.1 = (bf16[144,128]{1,0:T(8,128)(2,1)S(1)}, bf16[144,128]{1,0:T(8,128)(2,1)S(1)}, u32[]{:S(2)}, u32[]{:S(2)}) collective-permute-start(bf16[144,128]{1,0:T(8,128)(2,1)S(1)} %get-tuple-element.33), channel_id=1, source_target_pairs={{1,2},{2,1},{3,4},{4,3},{5,6},{6,5},{7,8},{8,7},{9,10},{10,9},{11,... | collective-permute-start | bytes 110600 | tf_op jit(solution)/shard_map/ppermute | solution.py:434
  11.4 10.7 %all-to-all-start = ((bf16[8,24,128]{2,1,0:T(8,128)(2,1)}), bf16[8,24,128]{2,1,0:T(8,128)(2,1)S(1)}, u32[]{:S(2)}, u32[]{:S(2)}) async-start(bf16[8,24,128]{2,1,0:T(8,128)(2,1)} %get-tuple-element.37), calls=%async_computation | async-start | bytes 98304 | tf_op jit(solution)/shard_map/all_to_all | solution.py:479
  17.1 14.5 %collective-permute-start.2 = (bf16[3,8,16,128]{3,2,1,0:T(8,128)(2,1)S(1)}, bf16[3,8,16,128]{3,2,1,0:T(8,128)(2,1)S(1)}, u32[]{:S(2)}, u32[]{:S(2)}) collective-permute-start(bf16[3,8,16,128]{3,2,1,0:T(8,128)(2,1)S(1)} %get-tuple-element.41), channel_id=1, source_target_pairs={{32,0},{64,32},{96,64},{128,96},{160,128},{192,160},{224,192},{33,... | collective-permute-start | bytes 294920 | tf_op jit(solution)/shard_map/ppermute | solution.py:480
  40.0 8.1 %collective-permute-start.3 = (bf16[3,8,8,128]{3,2,1,0:T(8,128)(2,1)S(1)}, bf16[3,8,8,128]{3,2,1,0:T(8,128)(2,1)S(1)}, u32[]{:S(2)}, u32[]{:S(2)}) collective-permute-start(bf16[3,8,8,128]{3,2,1,0:T(8,128)(2,1)S(1)} %get-tuple-element.44), channel_id=1, source_target_pairs={{0,32},{32,64},{64,96},{96,128},{128,160},{160,192},{192,224},{1,3... | collective-permute-start | bytes 147464 | tf_op jit(solution)/shard_map/ppermute | solution.py:500

commit v5 on v4

--- a/solution.py
+++ b/solution.py
@@ -286,7 +286,7 @@
         step(acts[p % 2], p, acts[1 - p % 2] if p < pairs - 1 else None, p + 1)
 
 
-def predict(halves, w_mix, w_out, offset, total):
+def predict(halves, w_mix, w_out, offset, total, first_half=None):
     def mixed(i, g):
         rows = slice(g * 16, (g + 1) * 16)
         x = [ref[i, at : at + 8, rows, :].reshape(128, 256) for ref, at in halves]
@@ -301,15 +301,34 @@
             queued.append(mixed(*order[n + 3]))
         h = 0.5 * now
         outer = (h * jnp.tanh(h) + h).astype(BF16)
+        lanes = slice(0, 256)
+        if first_half is not None:
+            first_half[i, g] = outer[:128]
+            outer = outer[128:]
+            lanes = slice(128, 256)
         if g % 2 == 0:
             held = outer
             continue
-        w = jnp.concatenate([w_out[g - 1], w_out[g]], axis=1)
+        w = jnp.concatenate([w_out[g - 1, :, lanes], w_out[g, :, lanes]], axis=1)
         p = jnp.dot(w, jnp.concatenate([held, outer], axis=0), preferred_element_type=F32)
         acc = p if g == 1 else acc + p
         if g == 7:
-            for e in range(2):
-                total[2 * i + e] = acc[:, e * 128 : (e + 1) * 128] + offset[...]
+            store(acc, offset, total, i)
+
+
+def store(acc, offset, total, i):
+    for e in range(2):
+        total[2 * i + e] = acc[:, e * 128 : (e + 1) * 128] + offset[...]
+
+
+def project_half(first_half, w_out, offset, total):
+    for i in range(4):
+        for g in range(0, 8, 2):
+            w = jnp.concatenate([w_out[g, :, 0:128], w_out[g + 1, :, 0:128]], axis=1)
+            x = first_half[i, g : g + 2].reshape(256, 256)
+            p = jnp.dot(w, x, preferred_element_type=F32)
+            acc = p if g == 0 else acc + p
+        store(acc, offset, total, i)
 
 
 def unorder(total, maps, rows):
@@ -342,7 +361,7 @@
 
 def late_kernel(
     offset, ahead, lifted, gain, w_in, w_mid, maps, w_mix, w_out, own,
-    send, near, inputs, act0, act1, spatial, total, rows,
+    send, kept, inputs, act0, act1, spatial, total, rows,
 ):
     def frame(f):
         x = [ahead[ch, f].astype(F32) for ch in range(3)]
@@ -350,17 +369,20 @@
         return tiles_of(noisy, edge, lifted[f * 8 : f * 8 + 8, :])
 
     network(inputs, 4, frame, maps, w_in, w_mid, gains(gain), act0, act1, spatial)
-    predict([(own, 8), (spatial, 0)], w_mix, w_out, offset, total)
+    predict([(own, 8), (spatial, 0)], w_mix, w_out, offset, total, kept)
     unorder(total, maps, rows)
     for f in range(8):
         w = ahead[0, f].astype(F32)
         share = w[15:16] / jnp.maximum(w[14:15] + w[15:16], 1.0)
         for o in range(3):
-            near[o, f] = picture(rows, o, f)
             send[o, f] = (picture(rows, o, f + 8) * share).astype(BF16)
 
 
-def early_kernel(offset, shares, maps, w_mix, w_out, own, near, mine, total, rows):
+def early_kernel(
+    offset, shares, maps, w_mix, w_out, own, kept, mine, total, rows, total_next, rows_next
+):
+    project_half(kept, w_out, offset, total_next)
+    unorder(total_next, maps, rows_next)
     predict([(own, 0), (own, 8)], w_mix, w_out, offset, total)
     unorder(total, maps, rows)
     for f in range(16):
@@ -369,7 +391,7 @@
             if f < 8:
                 mine[o, f] = picture(rows, o, f) * lead
             else:
-                mine[o, f] = near[o, f - 8] * lead + picture(rows, o, f) * trail
+                mine[o, f] = picture(rows_next, o, f - 8) * lead + picture(rows, o, f) * trail
 
 
 def join_kernel(mine, arrived, out):
@@ -488,12 +510,12 @@
         network_scratch(16),
         flops=10**10,
     )
-    send, next_half = call(
+    send, kept = call(
         late_kernel,
         "late",
         [],
         [offset, ahead, lifted_ahead, gain, w_in, w_mid, maps, w_mix, w_out, spatial],
-        (shape((3, 8, 8, 128), BF16), shape((3, 8, 8, 128), F32)),
+        (shape((3, 8, 8, 128), BF16), shape((4, 8, 128, 256), BF16)),
         network_scratch(8) + [pltpu.VMEM((4, 8, 128, 256), BF16)] + PICTURES,
         flops=10**10,
     )
@@ -502,9 +524,9 @@
         early_kernel,
         "early",
         [],
-        [offset, shares, maps, w_mix, w_out, spatial, next_half],
+        [offset, shares, maps, w_mix, w_out, spatial, kept],
         (shape((3, 16, 8, 128), F32),),
-        PICTURES,
+        PICTURES + PICTURES,
         flops=5 * 10**9,
     )
     (out,) = call(join_kernel, "join", [], [mine, arrived], (shape((3, 16, 8, 128), F32),))

time: 49.1 us -> 48.8 us (level)
  waiting for transfers between devices: 4.73 us -> 4.2 us
    ppermute x1, waiting for transfers between devices: 2.23 us -> 1.69 us  [body(): arrived = lax.ppermute(send, 'tm', forth)]
  transfers between devices with their start and end apart: 5 -> 5, of which waited for: 3 -> 3; matrix products, arithmetic and copies ran while one was open for 0% -> 0% of each run, Pallas kernels for 31% -> 32%
where the time goes in v5:
time: 48.8 us; the launch traced here: 48.5 us
  Pallas kernels  26.3 us (54%)
  starting transfers between devices  18 us (37%)
  waiting for transfers between devices  4.2 us (9%)
    pallas_call x6, Pallas kernels, call(): pl.pallas_call(kernel, out_shape=outs, in_specs=[SMEM] * len(scalars) + [...  25.6 us
    all_to_all x1, starting transfers between devices, body(): queue = lax.all_to_all(ask, 'tm', 0, 0, tiled=True)  5.76 us
    ppermute x1, starting transfers between devices, body(): from_far = lax.ppermute(to_far, 'rows', far)  5 us
    ppermute x1, starting transfers between devices, body(): ahead = lax.ppermute(pack, 'tm', back)  4.57 us
    ppermute x1, starting transfers between devices, body(): arrived = lax.ppermute(send, 'tm', forth)  2.53 us
    ppermute x1, waiting for transfers between devices, body(): from_far = lax.ppermute(to_far, 'rows', far)  2.17 us
    ppermute x1, waiting for transfers between devices, body(): arrived = lax.ppermute(send, 'tm', forth)  1.69 us
  transfers between devices with their start and end apart: 5, of which 3 were waited for; matrix products, arithmetic and copies ran while one was open for 0% of the time, Pallas kernels for 32%

profile of v5, /device:TPU:160, one launch (start us, length us, event | category | flops | bytes accessed | tf_op | source)
XLA Modules:
  0.0 48.5 jit_solution(4550366816066498422)
XLA Ops:
  0.0 0.0 copy-start
  0.0 1.1 %pack.1 = (bf16[144,128]{1,0:T(8,128)(2,1)S(1)}, bf16[144,128]{1,0:T(8,128)(2,1)S(1)}, bf16[48,128]{1,0:T(8,128)(2,1)S(1)}, bf16[3,16,8,128]{3,2,1,0:T(8,128)(2,1)S(1)}) custom-call(bf16[3,16,8,128]{3,2,1,0:T(8,128)(2,1)} %own_hbm.1, bf16[3,16,16]{2,1,0:T(8,128)(2,1)} %bitcast.15), custom_call_target="tpu_custom_call" | custom-call | flops 100000000 | bytes 1000000 | tf_op jit(solution)/shard_map/pack/pallas_call | solution.py:417
  1.1 0.1 collective-permute-start
  1.2 5.0 %collective-permute-start.1 = (bf16[144,128]{1,0:T(8,128)(2,1)S(1)}, bf16[144,128]{1,0:T(8,128)(2,1)S(1)}, u32[]{:S(2)}, u32[]{:S(2)}) collective-permute-start(bf16[144,128]{1,0:T(8,128)(2,1)S(1)} %get-tuple-element.33), channel_id=1, source_target_pairs={{1,2},{2,1},{3,4},{4,3},{5,6},{6,5},{7,8},{8,7},{9,10},{10,9},{11,... | collective-permute-start | bytes 110600 | tf_op jit(solution)/shard_map/ppermute | solution.py:456
  6.2 2.3 %prepare.1 = (bf16[5,256,256]{2,1,0:T(8,128)(2,1)S(1)}, bf16[256,1536]{1,0:T(8,128)(2,1)S(1)}, bf16[8,256,256]{2,1,0:T(8,128)(2,1)S(1)}, bf16[8,48,256]{2,1,0:T(...) custom-call(bf16[10,256,72]{2,1,0:T(8,128)(2,1)} %constant.4.clone.r, ...), custom_call_target="tpu_custom_call" | custom-call | flops 2000000000 | bytes 1000000 | tf_op jit(solution)/shard_map/prepare/pallas_call | solution.py:417
  8.5 0.0 collective-permute-done.near
  8.5 2.2 %collective-permute-done.1.far = bf16[144,128]{1,0:T(8,128)(2,1)S(1)} collective-permute-done((bf16[144,128]{1,0:T(8,128)(2,1)S(1)}, bf16[144,128]{1,0:T(8,128)(2,1)S(1)}, u32[]{:S(2)}, u32[]{:S(2)}) %collective-permute-start.1) | collective-permute-done | bytes 36896 | tf_op jit(solution)/shard_map/ppermute | solution.py:456
  10.7 0.7 %middle.1 = (bf16[3,16,8,128]{3,2,1,0:T(8,128)(2,1)S(1)}, bf16[8,24,128]{2,1,0:T(8,128)(2,1)}, bf16[3,8,16,128]{3,2,1,0:T(8,128)(2,1)S(1)}) custom-call(bf16[3,16,8,128]{3,2,1,0:T(8,128)(2,1)S(1)} %get-tuple-element.31.own, bf16[144,128]{1,0:T(8,128)(2,1)S(1)} %collective-permute-done.near, bf16[144,128]{1,0:T(8,128)(2,1)S(1)} %collective-permute-done.1.far, ...), custom_call_target="tpu_custom_call" | custom-call | tf_op jit(solution)/shard_map/middle/pallas_call | solution.py:492
  11.4 5.8 %all-to-all-start = ((bf16[8,24,128]{2,1,0:T(8,128)(2,1)}), bf16[8,24,128]{2,1,0:T(8,128)(2,1)S(1)}, u32[]{:S(2)}, u32[]{:S(2)}) async-start(bf16[8,24,128]{2,1,0:T(8,128)(2,1)} %get-tuple-element.37), calls=%async_computation | async-start | bytes 98304 | tf_op jit(solution)/shard_map/all_to_all | solution.py:501
  17.1 4.6 %collective-permute-start.2 = (bf16[3,8,16,128]{3,2,1,0:T(8,128)(2,1)S(1)}, bf16[3,8,16,128]{3,2,1,0:T(8,128)(2,1)S(1)}, u32[]{:S(2)}, u32[]{:S(2)}) collective-permute-start(bf16[3,8,16,128]{3,2,1,0:T(8,128)(2,1)S(1)} %get-tuple-element.41), channel_id=1, source_target_pairs={{32,0},{64,32},{96,64},{128,96},{160,128},{192,160},{224,192},{33,... | collective-permute-start | bytes 294920 | tf_op jit(solution)/shard_map/ppermute | solution.py:502
  21.7 0.3 all-to-all-done.queue
  22.0 0.0 copy-done
  22.0 9.6 %own.1 = (bf16[4,16,128,256]{3,2,1,0:T(8,128)(2,1)S(1)}, f32[64,384]{1,0:T(8,128)S(1)}) custom-call(bf16[192,384]{1,0:T(8,128)(2,1)S(1)} %get-tuple-element.30.hot, bf16[3,16,8,128]{3,2,1,0:T(8,128)(2,1)S(1)} %get-tuple-element.31.own, bf16[3,16,8,128]{3,2,1,0:T(8,128)(2,1)S(1)} %get-tuple-element.36.rim, bf16[8,24,128]{2,1,0:T(8,128)(2,1)S(1)} %all-to-all-done.queue, ...), custom_call_target="tpu_custom_call" | custom-call | flops 10000000000 | bytes 1000000 | tf_op jit(solution)/shard_map/own/pallas_call | solution.py:417
  31.7 0.0 collective-permute-done.2.ahead
  31.7 8.1 %late.1 = (bf16[3,8,8,128]{3,2,1,0:T(8,128)(2,1)S(1)}, bf16[4,8,128,256]{3,2,1,0:T(8,128)(2,1)S(1)}) custom-call(f32[48,128]{1,0:T(8,128)S(1)} %get-tuple-element.25.offset, bf16[3,8,16,128]{3,2,1,0:T(8,128)(2,1)S(1)} %collective-permute-done.2.ahead, f32[64,384]{1,0:T(8,128)S(1)} %get-tuple-element.42.lifted, f32[1,128]{1,0:T(1,128)S(1)} %bitcast.11, ...), custom_call_target="tpu_custom_call" | custom-call | flops 10000000000 | bytes 1000000 | tf_op jit(solution)/shard_map/late/pallas_call | solution.py:417
  39.7 2.5 %collective-permute-start.3 = (bf16[3,8,8,128]{3,2,1,0:T(8,128)(2,1)S(1)}, bf16[3,8,8,128]{3,2,1,0:T(8,128)(2,1)S(1)}, u32[]{:S(2)}, u32[]{:S(2)}) collective-permute-start(bf16[3,8,8,128]{3,2,1,0:T(8,128)(2,1)S(1)} %get-tuple-element.44), channel_id=1, source_target_pairs={{0,32},{32,64},{64,96},{96,128},{128,160},{160,192},{192,224},{1,3... | collective-permute-start | bytes 147464 | tf_op jit(solution)/shard_map/ppermute | solution.py:522
  42.3 3.9 %early.1.mine = f32[3,16,8,128]{3,2,1,0:T(8,128)S(1)} custom-call(f32[48,128]{1,0:T(8,128)S(1)} %get-tuple-element.25.offset, f32[32,128]{1,0:T(8,128)S(1)} %get-tuple-element.26.shares, bf16[128,896]{1,0:T(8,128)(2,1)S(1)} %get-tuple-element.27.maps, bf16[8,256,256]{2,1,0:T(8,128)(2,1)S(1)} %get-tuple-element.28.w_mix, ...), custom_call_target="tpu_custom_call" | custom-call | flops 5000000000 | bytes 1000000 | tf_op jit(solution)/shard_map/early/pallas_call | solution.py:417
  46.1 1.7 %collective-permute-done.3.arrived = bf16[3,8,8,128]{3,2,1,0:T(8,128)(2,1)S(1)} collective-permute-done((bf16[3,8,8,128]{3,2,1,0:T(8,128)(2,1)S(1)}, bf16[3,8,8,128]{3,2,1,0:T(8,128)(2,1)S(1)}, u32[]{:S(2)}, u32[]{:S(2)}) %collective-permute-start.3) | collective-permute-done | bytes 49184 | tf_op jit(solution)/shard_map/ppermute | solution.py:522
  47.8 0.7 %join.1 = f32[3,16,8,128]{3,2,1,0:T(8,128)} custom-call(f32[3,16,8,128]{3,2,1,0:T(8,128)S(1)} %early.1.mine, bf16[3,8,8,128]{3,2,1,0:T(8,128)(2,1)S(1)} %collective-permute-done.3.arrived), custom_call_target="tpu_custom_call" | custom-call | flops 100000000 | bytes 1000000 | tf_op jit(solution)/shard_map/join/pallas_call | solution.py:417
Async XLA Ops:
  0.0 22.0 %copy-start = (f32[128]{0:T(128)S(1)}, f32[128]{0:T(128)}, u32[]{:S(2)}) copy-start(f32[128]{0:T(128)} %param.19) | copy-start | bytes 1540
  1.1 7.4 %collective-permute-start = (bf16[144,128]{1,0:T(8,128)(2,1)S(1)}, bf16[144,128]{1,0:T(8,128)(2,1)S(1)}, u32[]{:S(2)}, u32[]{:S(2)}) collective-permute-start(bf16[144,128]{1,0:T(8,128)(2,1)S(1)} %get-tuple-element.32), channel_id=1, source_target_pairs={{0,1},{1,0},{2,3},{3,2},{4,5},{5,4},{6,7},{7,6},{8,9},{9,8},{10,11... | collective-permute-start | bytes 110600 | tf_op jit(solution)/shard_map/ppermute | solution.py:457
  1.2 9.5 %collective-permute-start.1 = (bf16[144,128]{1,0:T(8,128)(2,1)S(1)}, bf16[144,128]{1,0:T(8,128)(2,1)S(1)}, u32[]{:S(2)}, u32[]{:S(2)}) collective-permute-start(bf16[144,128]{1,0:T(8,128)(2,1)S(1)} %get-tuple-element.33), channel_id=1, source_target_pairs={{1,2},{2,1},{3,4},{4,3},{5,6},{6,5},{7,8},{8,7},{9,10},{10,9},{11,... | collective-permute-start | bytes 110600 | tf_op jit(solution)/shard_map/ppermute | solution.py:456
  11.4 10.7 %all-to-all-start = ((bf16[8,24,128]{2,1,0:T(8,128)(2,1)}), bf16[8,24,128]{2,1,0:T(8,128)(2,1)S(1)}, u32[]{:S(2)}, u32[]{:S(2)}) async-start(bf16[8,24,128]{2,1,0:T(8,128)(2,1)} %get-tuple-element.37), calls=%async_computation | async-start | bytes 98304 | tf_op jit(solution)/shard_map/all_to_all | solution.py:501
  17.1 14.5 %collective-permute-start.2 = (bf16[3,8,16,128]{3,2,1,0:T(8,128)(2,1)S(1)}, bf16[3,8,16,128]{3,2,1,0:T(8,128)(2,1)S(1)}, u32[]{:S(2)}, u32[]{:S(2)}) collective-permute-start(bf16[3,8,16,128]{3,2,1,0:T(8,128)(2,1)S(1)} %get-tuple-element.41), channel_id=1, source_target_pairs={{32,0},{64,32},{96,64},{128,96},{160,128},{192,160},{224,192},{33,... | collective-permute-start | bytes 294920 | tf_op jit(solution)/shard_map/ppermute | solution.py:502
  39.7 8.1 %collective-permute-start.3 = (bf16[3,8,8,128]{3,2,1,0:T(8,128)(2,1)S(1)}, bf16[3,8,8,128]{3,2,1,0:T(8,128)(2,1)S(1)}, u32[]{:S(2)}, u32[]{:S(2)}) collective-permute-start(bf16[3,8,8,128]{3,2,1,0:T(8,128)(2,1)S(1)} %get-tuple-element.44), channel_id=1, source_target_pairs={{0,32},{32,64},{64,96},{96,128},{128,160},{160,192},{192,224},{1,3... | collective-permute-start | bytes 147464 | tf_op jit(solution)/shard_map/ppermute | solution.py:522

commit v6 on v5

--- a/solution.py
+++ b/solution.py
@@ -346,17 +346,17 @@
 
 
 def own_kernel(
-    hot, own, rim, queue, gain, w_in, w_mid, maps, spatial, lifted_ahead, inputs, act0, act1
+    hot, own, rim, queue, gain, w_in, w_mid, maps, spatial, lifted, inputs, act0, act1
 ):
-    lifted = lift(hot, queue, maps)
-    lifted_ahead[...] = lifted[128:]
+    base = lift(hot, queue, maps)
+    lifted[...] = base
 
     def frame(f):
-        noisy = [own[ch, f].astype(F32) for ch in range(3)]
-        edge = [rim[ch, f].astype(F32) for ch in range(3)]
-        return tiles_of(noisy, edge, lifted[f * 8 : f * 8 + 8])
-
-    network(inputs, 8, frame, maps, w_in, w_mid, gains(gain), act0, act1, spatial)
+        noisy = [own[ch, f + 8].astype(F32) for ch in range(3)]
+        edge = [rim[ch, f + 8].astype(F32) for ch in range(3)]
+        return tiles_of(noisy, edge, base[f * 8 + 64 : f * 8 + 72])
+
+    network(inputs, 4, frame, maps, w_in, w_mid, gains(gain), act0, act1, spatial)
 
 
 def late_kernel(
@@ -366,10 +366,10 @@
     def frame(f):
         x = [ahead[ch, f].astype(F32) for ch in range(3)]
         noisy, edge = [tile[:8] for tile in x], [tile[8:] for tile in x]
-        return tiles_of(noisy, edge, lifted[f * 8 : f * 8 + 8, :])
+        return tiles_of(noisy, edge, lifted[f * 8 + 128 : f * 8 + 136, :])
 
     network(inputs, 4, frame, maps, w_in, w_mid, gains(gain), act0, act1, spatial)
-    predict([(own, 8), (spatial, 0)], w_mix, w_out, offset, total, kept)
+    predict([(own, 0), (spatial, 0)], w_mix, w_out, offset, total, kept)
     unorder(total, maps, rows)
     for f in range(8):
         w = ahead[0, f].astype(F32)
@@ -379,11 +379,18 @@
 
 
 def early_kernel(
-    offset, shares, maps, w_mix, w_out, own, kept, mine, total, rows, total_next, rows_next
+    offset, shares, frames, rim, lifted, gain, w_in, w_mid, maps, w_mix, w_out, own, kept,
+    mine, inputs, act0, act1, spatial, total, rows, total_next, rows_next,
 ):
+    def frame(f):
+        noisy = [frames[ch, f].astype(F32) for ch in range(3)]
+        edge = [rim[ch, f].astype(F32) for ch in range(3)]
+        return tiles_of(noisy, edge, lifted[f * 8 : f * 8 + 8, :])
+
+    network(inputs, 4, frame, maps, w_in, w_mid, gains(gain), act0, act1, spatial)
     project_half(kept, w_out, offset, total_next)
     unorder(total_next, maps, rows_next)
-    predict([(own, 0), (own, 8)], w_mix, w_out, offset, total)
+    predict([(spatial, 0), (own, 0)], w_mix, w_out, offset, total)
     unorder(total, maps, rows)
     for f in range(16):
         lead, trail = shares[f : f + 1, :], shares[f + 16 : f + 17, :]
@@ -501,20 +508,20 @@
     queue = lax.all_to_all(ask, "tm", 0, 0, tiled=True)
     ahead = lax.ppermute(pack, "tm", back)
     gain = gain_mid.reshape(1, 128)
-    spatial, lifted_ahead = call(
+    spatial, lifted = call(
         own_kernel,
         "own",
         [],
         [hot, own, rim, queue, gain, w_in, w_mid, maps],
-        (shape((4, 16, 128, 256), BF16), shape((64, 384), F32)),
-        network_scratch(16),
+        (shape((4, 8, 128, 256), BF16), shape((192, 384), F32)),
+        network_scratch(8),
         flops=10**10,
     )
     send, kept = call(
         late_kernel,
         "late",
         [],
-        [offset, ahead, lifted_ahead, gain, w_in, w_mid, maps, w_mix, w_out, spatial],
+        [offset, ahead, lifted, gain, w_in, w_mid, maps, w_mix, w_out, spatial],
         (shape((3, 8, 8, 128), BF16), shape((4, 8, 128, 256), BF16)),
         network_scratch(8) + [pltpu.VMEM((4, 8, 128, 256), BF16)] + PICTURES,
         flops=10**10,
@@ -524,10 +531,10 @@
         early_kernel,
         "early",
         [],
-        [offset, shares, maps, w_mix, w_out, spatial, kept],
+        [offset, shares, own, rim, lifted, gain, w_in, w_mid, maps, w_mix, w_out, spatial, kept],
         (shape((3, 16, 8, 128), F32),),
-        PICTURES + PICTURES,
-        flops=5 * 10**9,
+        network_scratch(8) + [pltpu.VMEM((4, 8, 128, 256), BF16)] + PICTURES + PICTURES,
+        flops=10**10,
     )
     (out,) = call(join_kernel, "join", [], [mine, arrived], (shape((3, 16, 8, 128), F32),))
     return out

time: 48.8 us -> 47.9 us (0.982)
  the two profiles are of different devices: /device:TPU:160 before, /device:TPU:95 now
where the time goes in v6:
time: 47.9 us; the launch traced here: 47.6 us
  Pallas kernels  26.4 us (55%)
  starting transfers between devices  18.6 us (39%)
  waiting for transfers between devices  2.44 us (5%)
    pallas_call x6, Pallas kernels, call(): pl.pallas_call(kernel, out_shape=outs, in_specs=[SMEM] * len(scalars) + [...  25.7 us
    ppermute x1, starting transfers between devices, body(): from_far = lax.ppermute(to_far, 'rows', far)  5.67 us
    all_to_all x1, starting transfers between devices, body(): queue = lax.all_to_all(ask, 'tm', 0, 0, tiled=True)  5.57 us
    ppermute x1, starting transfers between devices, body(): arrived = lax.ppermute(send, 'tm', forth)  4.16 us
    ppermute x1, starting transfers between devices, body(): ahead = lax.ppermute(pack, 'tm', back)  2.47 us
    ppermute x1, waiting for transfers between devices, body(): from_far = lax.ppermute(to_far, 'rows', far)  1.48 us
  transfers between devices with their start and end apart: 5, of which 2 were waited for; matrix products, arithmetic and copies ran while one was open for 0% of the time, Pallas kernels for 34%

profile of v6, /device:TPU:95, one launch (start us, length us, event | category | flops | bytes accessed | tf_op | source)
XLA Modules:
  0.0 47.6 jit_solution(14839414432031776592)
XLA Ops:
  0.0 1.1 %pack.1 = (bf16[144,128]{1,0:T(8,128)(2,1)S(1)}, bf16[144,128]{1,0:T(8,128)(2,1)S(1)}, bf16[48,128]{1,0:T(8,128)(2,1)S(1)}, bf16[3,16,8,128]{3,2,1,0:T(8,128)(2,1)S(1)}) custom-call(bf16[3,16,8,128]{3,2,1,0:T(8,128)(2,1)} %own_hbm.1, bf16[3,16,16]{2,1,0:T(8,128)(2,1)} %bitcast.16), custom_call_target="tpu_custom_call" | custom-call | flops 100000000 | bytes 1000000 | tf_op jit(solution)/shard_map/pack/pallas_call | solution.py:424
  1.1 0.8 %collective-permute-start = (bf16[144,128]{1,0:T(8,128)(2,1)S(1)}, bf16[144,128]{1,0:T(8,128)(2,1)S(1)}, u32[]{:S(2)}, u32[]{:S(2)}) collective-permute-start(bf16[144,128]{1,0:T(8,128)(2,1)S(1)} %get-tuple-element.28), channel_id=1, source_target_pairs={{0,1},{1,0},{2,3},{3,2},{4,5},{5,4},{6,7},{7,6},{8,9},{9,8},{10,11... | collective-permute-start | bytes 110600 | tf_op jit(solution)/shard_map/ppermute | solution.py:464
  1.8 5.7 %collective-permute-start.1 = (bf16[144,128]{1,0:T(8,128)(2,1)S(1)}, bf16[144,128]{1,0:T(8,128)(2,1)S(1)}, u32[]{:S(2)}, u32[]{:S(2)}) collective-permute-start(bf16[144,128]{1,0:T(8,128)(2,1)S(1)} %get-tuple-element.29), channel_id=1, source_target_pairs={{1,2},{2,1},{3,4},{4,3},{5,6},{6,5},{7,8},{8,7},{9,10},{10,9},{11,... | collective-permute-start | bytes 110600 | tf_op jit(solution)/shard_map/ppermute | solution.py:463
  7.5 0.0 copy-start
  7.5 2.3 %prepare.1 = (bf16[5,256,256]{2,1,0:T(8,128)(2,1)S(1)}, bf16[256,1536]{1,0:T(8,128)(2,1)S(1)}, bf16[8,256,256]{2,1,0:T(8,128)(2,1)S(1)}, bf16[8,48,256]{2,1,0:T(...) custom-call(bf16[10,256,72]{2,1,0:T(8,128)(2,1)} %constant.4.clone.r, ...), custom_call_target="tpu_custom_call" | custom-call | flops 2000000000 | bytes 1000000 | tf_op jit(solution)/shard_map/prepare/pallas_call | solution.py:424
  9.8 0.0 collective-permute-done.near
  9.8 1.5 %collective-permute-done.1.far = bf16[144,128]{1,0:T(8,128)(2,1)S(1)} collective-permute-done((bf16[144,128]{1,0:T(8,128)(2,1)S(1)}, bf16[144,128]{1,0:T(8,128)(2,1)S(1)}, u32[]{:S(2)}, u32[]{:S(2)}) %collective-permute-start.1) | collective-permute-done | bytes 36896 | tf_op jit(solution)/shard_map/ppermute | solution.py:463
  11.3 0.7 %middle.1 = (bf16[3,16,8,128]{3,2,1,0:T(8,128)(2,1)S(1)}, bf16[8,24,128]{2,1,0:T(8,128)(2,1)}, bf16[3,8,16,128]{3,2,1,0:T(8,128)(2,1)S(1)}) custom-call(bf16[3,16,8,128]{3,2,1,0:T(8,128)(2,1)S(1)} %get-tuple-element.27.own.frames, bf16[144,128]{1,0:T(8,128)(2,1)S(1)} %collective-permute-done.near, bf16[144,128]{1,0:T(8,128)(2,1)S(1)} %collective-permute-done.1.far, ...), custom_call_target="tpu_custom_call" | custom-call | tf_op jit(solution)/shard_map/middle/pallas_call | solution.py:499
  12.0 5.6 %all-to-all-start = ((bf16[8,24,128]{2,1,0:T(8,128)(2,1)}), bf16[8,24,128]{2,1,0:T(8,128)(2,1)S(1)}, u32[]{:S(2)}, u32[]{:S(2)}) async-start(bf16[8,24,128]{2,1,0:T(8,128)(2,1)} %get-tuple-element.34), calls=%async_computation | async-start | bytes 98304 | tf_op jit(solution)/shard_map/all_to_all | solution.py:508
  17.6 2.5 %collective-permute-start.2 = (bf16[3,8,16,128]{3,2,1,0:T(8,128)(2,1)S(1)}, bf16[3,8,16,128]{3,2,1,0:T(8,128)(2,1)S(1)}, u32[]{:S(2)}, u32[]{:S(2)}) collective-permute-start(bf16[3,8,16,128]{3,2,1,0:T(8,128)(2,1)S(1)} %get-tuple-element.42), channel_id=1, source_target_pairs={{32,0},{64,32},{96,64},{128,96},{160,128},{192,160},{224,192},{33,... | collective-permute-start | bytes 294920 | tf_op jit(solution)/shard_map/ppermute | solution.py:509
  20.1 1.0 %all-to-all-done.queue = bf16[8,24,128]{2,1,0:T(8,128)(2,1)S(1)} async-done(((bf16[8,24,128]{2,1,0:T(8,128)(2,1)}), bf16[8,24,128]{2,1,0:T(8,128)(2,1)S(1)}, u32[]{:S(2)}, u32[]{:S(2)}) %all-to-all-start) | async-done | bytes 49184 | tf_op jit(solution)/shard_map/all_to_all | solution.py:508
  21.0 0.0 copy-done
  21.0 5.2 %own.1 = (bf16[4,8,128,256]{3,2,1,0:T(8,128)(2,1)S(1)}, f32[192,384]{1,0:T(8,128)S(1)}) custom-call(bf16[192,384]{1,0:T(8,128)(2,1)S(1)} %get-tuple-element.33.hot, bf16[3,16,8,128]{3,2,1,0:T(8,128)(2,1)S(1)} %get-tuple-element.27.own.frames, bf16[3,16,8,128]{3,2,1,0:T(8,128)(2,1)S(1)} %get-tuple-element.32.rim, bf16[8,24,128]{2,1,0:T(8,128)(2,1)S(1)} %all-to-all-done.queue, ...), custom_call_target="tpu_custom_call" | custom-call | flops 10000000000 | bytes 1000000 | tf_op jit(solution)/shard_map/own/pallas_call | solution.py:424
  26.3 0.0 collective-permute-done.2.ahead
  26.3 7.8 %late.1 = (bf16[3,8,8,128]{3,2,1,0:T(8,128)(2,1)S(1)}, bf16[4,8,128,256]{3,2,1,0:T(8,128)(2,1)S(1)}) custom-call(f32[48,128]{1,0:T(8,128)S(1)} %get-tuple-element.25.offset, bf16[3,8,16,128]{3,2,1,0:T(8,128)(2,1)S(1)} %collective-permute-done.2.ahead, f32[192,384]{1,0:T(8,128)S(1)} %get-tuple-element.38.lifted, f32[1,128]{1,0:T(1,128)S(1)} %bitcast.11, ...), custom_call_target="tpu_custom_call" | custom-call | flops 10000000000 | bytes 1000000 | tf_op jit(solution)/shard_map/late/pallas_call | solution.py:424
  34.1 4.2 %collective-permute-start.3 = (bf16[3,8,8,128]{3,2,1,0:T(8,128)(2,1)S(1)}, bf16[3,8,8,128]{3,2,1,0:T(8,128)(2,1)S(1)}, u32[]{:S(2)}, u32[]{:S(2)}) collective-permute-start(bf16[3,8,8,128]{3,2,1,0:T(8,128)(2,1)S(1)} %get-tuple-element.44), channel_id=1, source_target_pairs={{0,32},{32,64},{64,96},{96,128},{128,160},{160,192},{192,224},{1,3... | collective-permute-start | bytes 147464 | tf_op jit(solution)/shard_map/ppermute | solution.py:529
  38.2 8.6 %early.1.mine = f32[3,16,8,128]{3,2,1,0:T(8,128)S(1)} custom-call(f32[48,128]{1,0:T(8,128)S(1)} %get-tuple-element.25.offset, f32[32,128]{1,0:T(8,128)S(1)} %get-tuple-element.26.shares, bf16[3,16,8,128]{3,2,1,0:T(8,128)(2,1)S(1)} %get-tuple-element.27.own.frames, bf16[3,16,8,128]{3,2,1,0:T(8,128)(2,1)S(1)} %get-tuple-element.32.rim, ...), custom_call_target="tpu_custom_call" | custom-call | flops 10000000000 | bytes 1000000 | tf_op jit(solution)/shard_map/early/pallas_call | solution.py:424
  46.9 0.0 collective-permute-done.3.arrived
  46.9 0.7 %join.1 = f32[3,16,8,128]{3,2,1,0:T(8,128)} custom-call(f32[3,16,8,128]{3,2,1,0:T(8,128)S(1)} %early.1.mine, bf16[3,8,8,128]{3,2,1,0:T(8,128)(2,1)S(1)} %collective-permute-done.3.arrived), custom_call_target="tpu_custom_call" | custom-call | flops 100000000 | bytes 1000000 | tf_op jit(solution)/shard_map/join/pallas_call | solution.py:424
Async XLA Ops:
  1.1 8.8 %collective-permute-start = (bf16[144,128]{1,0:T(8,128)(2,1)S(1)}, bf16[144,128]{1,0:T(8,128)(2,1)S(1)}, u32[]{:S(2)}, u32[]{:S(2)}) collective-permute-start(bf16[144,128]{1,0:T(8,128)(2,1)S(1)} %get-tuple-element.28), channel_id=1, source_target_pairs={{0,1},{1,0},{2,3},{3,2},{4,5},{5,4},{6,7},{7,6},{8,9},{9,8},{10,11... | collective-permute-start | bytes 110600 | tf_op jit(solution)/shard_map/ppermute | solution.py:464
  1.8 9.5 %collective-permute-start.1 = (bf16[144,128]{1,0:T(8,128)(2,1)S(1)}, bf16[144,128]{1,0:T(8,128)(2,1)S(1)}, u32[]{:S(2)}, u32[]{:S(2)}) collective-permute-start(bf16[144,128]{1,0:T(8,128)(2,1)S(1)} %get-tuple-element.29), channel_id=1, source_target_pairs={{1,2},{2,1},{3,4},{4,3},{5,6},{6,5},{7,8},{8,7},{9,10},{10,9},{11,... | collective-permute-start | bytes 110600 | tf_op jit(solution)/shard_map/ppermute | solution.py:463
  7.5 13.5 %copy-start = (f32[128]{0:T(128)S(1)}, f32[128]{0:T(128)}, u32[]{:S(2)}) copy-start(f32[128]{0:T(128)} %param.19) | copy-start | bytes 1540
  12.0 9.0 %all-to-all-start = ((bf16[8,24,128]{2,1,0:T(8,128)(2,1)}), bf16[8,24,128]{2,1,0:T(8,128)(2,1)S(1)}, u32[]{:S(2)}, u32[]{:S(2)}) async-start(bf16[8,24,128]{2,1,0:T(8,128)(2,1)} %get-tuple-element.34), calls=%async_computation | async-start | bytes 98304 | tf_op jit(solution)/shard_map/all_to_all | solution.py:508
  17.6 8.7 %collective-permute-start.2 = (bf16[3,8,16,128]{3,2,1,0:T(8,128)(2,1)S(1)}, bf16[3,8,16,128]{3,2,1,0:T(8,128)(2,1)S(1)}, u32[]{:S(2)}, u32[]{:S(2)}) collective-permute-start(bf16[3,8,16,128]{3,2,1,0:T(8,128)(2,1)S(1)} %get-tuple-element.42), channel_id=1, source_target_pairs={{32,0},{64,32},{96,64},{128,96},{160,128},{192,160},{224,192},{33,... | collective-permute-start | bytes 294920 | tf_op jit(solution)/shard_map/ppermute | solution.py:509
  34.1 12.8 %collective-permute-start.3 = (bf16[3,8,8,128]{3,2,1,0:T(8,128)(2,1)S(1)}, bf16[3,8,8,128]{3,2,1,0:T(8,128)(2,1)S(1)}, u32[]{:S(2)}, u32[]{:S(2)}) collective-permute-start(bf16[3,8,8,128]{3,2,1,0:T(8,128)(2,1)S(1)} %get-tuple-element.44), channel_id=1, source_target_pairs={{0,32},{32,64},{64,96},{96,128},{128,160},{160,192},{192,224},{1,3... | collective-permute-start | bytes 147464 | tf_op jit(solution)/shard_map/ppermute | solution.py:529
